TPU v7x, 32 devices: a whole 2x2x4 slice. The times are simulated.
32 devices in a mesh: dp: 16 (over z, x, core), tensor: 2 (over y).
Axes of the slice: x: 2, y: 2, z: 4, core: 2. Of those that a mesh axis runs over, the one named last changes fastest.
Arguments:
- tokens: bfloat16 [6144, 1024], P(('dp', 'tensor')), may hold values from -6 to 6
- cotangent: bfloat16 [6144, 1024], P(('dp', 'tensor')), may hold values from -6 to 6
- seq_lengths: int32 [16, 8], P('dp'), may hold values from 0 to 384, as said below
- norm1_gain: float32 [1024], replicated, may hold values from 0.5 to 1.5
- norm2_gain: float32 [1024], replicated, may hold values from 0.5 to 1.5
- mixer_in: bfloat16 [1024, 2, 1536], P(None, None, 'tensor'), may hold values from -0.1875 to 0.1875
- state_in: bfloat16 [1024, 256], replicated, may hold values from -0.1875 to 0.1875
- step_in: bfloat16 [1024, 24], P(None, 'tensor'), may hold values from -0.375 to 0.375
- conv_inner: float32 [4, 1536], P(None, 'tensor'), may hold values from -3 to 3
- conv_state: float32 [4, 256], replicated, may hold values from -3 to 3
- step_bias: float32 [24], P('tensor'), may hold values from -4 to -2
- decay_log: float32 [24], P('tensor'), may hold values from -3 to 0.5
- skip_gain: float32 [24], P('tensor'), may hold values from 0.5 to 1.5
- mixer_out: bfloat16 [1024, 1536], P(None, 'tensor'), may hold values from -0.4375 to 0.4375
- query_in: bfloat16 [1024, 512], P(None, 'tensor'), may hold values from -0.1875 to 0.1875
- key_value: bfloat16 [1024, 2, 128], replicated, may hold values from -0.1875 to 0.1875
- attend_out: bfloat16 [1024, 512], P(None, 'tensor'), may hold values from -2 to 2
- gate_up: bfloat16 [1024, 2, 2048], P(None, None, 'tensor'), may hold values from -0.1875 to 0.1875
- down_out: bfloat16 [1024, 2048], P(None, 'tensor'), may hold values from -0.125 to 0.125
Outputs:
- block_out: bfloat16 [6144, 1024], P(('dp', 'tensor'))
- token_grad: bfloat16 [6144, 1024], P(('dp', 'tensor'))
- grad_norm1: float32 [1024], replicated
- grad_norm2: float32 [1024], replicated
- grad_mixer_in: float32 [1024, 2, 1536], P('dp', None, 'tensor')
- grad_state_in: float32 [1024, 256], P('dp')
- grad_step_in: float32 [1024, 24], P('dp', 'tensor')
- grad_conv_inner: float32 [4, 1536], P(None, 'tensor')
- grad_conv_state: float32 [4, 256], replicated
- grad_step_bias: float32 [24], P('tensor')
- grad_decay_log: float32 [24], P('tensor')
- grad_skip_gain: float32 [24], P('tensor')
- grad_mixer_out: float32 [1024, 1536], P('dp', 'tensor')
- grad_query_in: float32 [1024, 512], P('dp', 'tensor')
- grad_key_value: float32 [1024, 2, 128], P('dp')
- grad_attend_out: float32 [1024, 512], P('dp', 'tensor')
- grad_gate_up: float32 [1024, 2, 2048], P('dp', None, 'tensor')
- grad_down_out: float32 [1024, 2048], P('dp', 'tensor')
Inputs may be any that keep to these rules, and one draw needn't show every extreme that they name: `seq_lengths`: row g lists the lengths of the sequences of data group g in the order they lie in its 384 slots, then zeros; a row has 1 to 8 sequences and its lengths sum to at least 192; in some row one sequence fills all 384 slots.
All inputs are finite; a program needn't handle non-finite values.
Results may differ from a plain program's by a relative error of at most 0.018.
Values may be sent and summed in bfloat16 or wider, within the bound.
No kernel may reach another device: no remote copies, remote signals or barrier semaphores. Data moves between devices by JAX's collectives and lax.ppermute only.
A program may use at most 128 MiB of HBM per device.

v0:
```python
import jax
import jax.numpy as jnp
from jax import lax
from jax.sharding import PartitionSpec as P

HD = 64
QH = 8
KVH = 2
SPAN = 128
ATT_ROWS = 384


rope_base = 100000000000.0
norm_eps = 1e-05
highest = lax.Precision.HIGHEST


def segments(lengths, row_count):
    seq_ends = jnp.cumsum(lengths)
    places = jnp.arange(row_count, dtype=jnp.int32)
    passed = places[:, None] >= seq_ends[None, :]
    seq_ids = jnp.sum(passed.astype(jnp.int32), axis=1)
    starts = jnp.max(jnp.where(passed, seq_ends[None, :], 0), axis=1)
    is_live = (places < seq_ends[-1]).astype(jnp.float32)
    return (seq_ids, places - starts, is_live)


def rms_scale(values, gain):
    factor = lax.rsqrt(jnp.mean(values * values, axis=-1, keepdims=True) + norm_eps)
    return values * factor * gain


def rotate(vectors, positions, sign):
    half_width = vectors.shape[-1] // 2
    frequency = rope_base ** (-2.0 * jnp.arange(half_width, dtype=jnp.float32) / vectors.shape[-1])
    angles = positions.astype(jnp.float32)[:, None, None] * frequency[None, None, :]
    cosine = jnp.cos(angles)
    sine_table = jnp.sin(angles)
    first_half = vectors[..., :half_width]
    second_half = vectors[..., half_width:]
    return jnp.concatenate(
        [
            first_half * cosine - sign * second_half * sine_table,
            second_half * cosine + sign * first_half * sine_table,
        ],
        axis=-1,
    )


def causal_conv(values, weight, seq_ids):
    row_count = values.shape[0]
    kernel_len = weight.shape[0]
    running = jnp.zeros(values.shape, jnp.float32)
    for tap_index in range(kernel_len):
        offset = kernel_len - 1 - tap_index
        shifted = jnp.pad(values, ((offset, 0), (0, 0)))[:row_count]
        owner_ids = jnp.pad(seq_ids, (offset, 0), constant_values=-1)[:row_count]
        running = (
            running
            + jnp.where((owner_ids == seq_ids)[:, None], shifted, 0.0) * weight[tap_index][None, :]
        )
    return running


def state_scan(inner_x, step_sizes, state_b, state_c, decay_rates, seq_ids, block_len):
    row_count, head_count, head_dim = inner_x.shape
    blocks = row_count // block_len
    prior_ids = jnp.concatenate([jnp.full((1,), -1, jnp.int32), seq_ids[:-1]])
    within = jnp.arange(block_len, dtype=jnp.int32)
    causal = within[:, None] >= within[None, :]

    def advance(carried, pieces):
        inner_b, steps_b, keys_b, reads_b, ids_b, before = pieces
        log_decay = jnp.cumsum(-steps_b * decay_rates[None, :], axis=0)
        linked = (ids_b[:, None] == ids_b[None, :]) & causal
        decays = jnp.exp(
            jnp.where(linked[:, :, None], log_decay[:, None, :] - log_decay[None, :, :], -jnp.inf)
        )
        intersection = jnp.dot(reads_b, keys_b.T, precision=highest)
        mixing = intersection[:, :, None] * decays * steps_b[None, :, :]
        inside = jnp.einsum("ijh,jhp->ihp", mixing, inner_b, precision=highest)
        keeps_state = (ids_b == before).astype(jnp.float32)
        from_state = jnp.einsum("in,hpn->ihp", reads_b, carried, precision=highest)
        outside = from_state * (jnp.exp(log_decay) * keeps_state[:, None])[:, :, None]
        tail_ok = (ids_b == ids_b[-1]).astype(jnp.float32)
        towards = jnp.exp(log_decay[-1][None, :] - log_decay) * tail_ok[:, None] * steps_b
        fresh_state = jnp.einsum(
            "jhp,jn->hpn", towards[:, :, None] * inner_b, keys_b, precision=highest
        )
        carry_on = jnp.exp(log_decay[-1]) * (ids_b[-1] == before).astype(jnp.float32)
        return (fresh_state + carry_on[:, None, None] * carried, inside + outside)

    pieces = (
        inner_x.reshape(blocks, block_len, head_count, head_dim),
        step_sizes.reshape(blocks, block_len, head_count),
        state_b.reshape(blocks, block_len, -1),
        state_c.reshape(blocks, block_len, -1),
        seq_ids.reshape(blocks, block_len),
        prior_ids[::block_len],
    )
    initial = jnp.zeros((head_count, head_dim, state_b.shape[1]), jnp.float32)
    final_state, result = lax.scan(jax.checkpoint(advance), initial, pieces)
    return result.reshape(row_count, head_count, head_dim)


def mamba_mixer(
    gate_z,
    inner_x,
    state_raw,
    step_raw,
    conv_inner,
    conv_state,
    step_bias,
    decay_log,
    skip_gain,
    seq_ids,
    block_len,
):
    row_count = inner_x.shape[0]
    head_count = step_raw.shape[1]
    state_dim = state_raw.shape[1] // 2
    conv_x = jax.nn.silu(causal_conv(inner_x, conv_inner, seq_ids)).reshape(
        row_count, head_count, -1
    )
    conv_bc = jax.nn.silu(causal_conv(state_raw, conv_state, seq_ids))
    step_sizes = jax.nn.softplus(step_raw + step_bias[None, :])
    scanned = state_scan(
        conv_x,
        step_sizes,
        conv_bc[:, :state_dim],
        conv_bc[:, state_dim:],
        jnp.exp(decay_log),
        seq_ids,
        block_len,
    )
    output = scanned + skip_gain[None, :, None] * conv_x
    return output.reshape(row_count, -1) * jax.nn.silu(gate_z)


def swiglu(gate_part, up_part):
    return jax.nn.silu(gate_part) * up_part


def product(left, right):
    return jnp.dot(left, right, preferred_element_type=jnp.float32)


def contract_last(left, right):
    return lax.dot_general(
        left, right, (((1,), (1,)), ((), ())), preferred_element_type=jnp.float32
    )


def contract_first(left, right):
    return lax.dot_general(
        left, right, (((0,), (0,)), ((), ())), preferred_element_type=jnp.float32
    )


def attend(queries, keys_b, values_b, seq_ids, block_rows):
    row_count = keys_b.shape[0]
    scaling = queries.shape[2] ** (-0.5)
    columns = jnp.arange(row_count, dtype=jnp.int32)

    def one_block(row_start):
        places = row_start + jnp.arange(block_rows, dtype=jnp.int32)
        allowed = (seq_ids[:, None] == seq_ids[None, :]) & (columns[None, :] <= places[:, None])
        scores = (
            jnp.einsum("ihd,jd->hij", queries, keys_b, preferred_element_type=jnp.float32) * scaling
        )
        scores = jnp.where(allowed[None], scores, -jnp.inf)
        row_max = jnp.max(scores, axis=-1, keepdims=True)
        exp_scores = jnp.exp(scores - row_max)
        row_total = jnp.sum(exp_scores, axis=-1, keepdims=True)
        probs_f = exp_scores / row_total
        mixed = jnp.einsum(
            "hij,jd->ihd",
            probs_f.astype(jnp.bfloat16),
            values_b,
            preferred_element_type=jnp.float32,
        )
        return (mixed, (row_max + jnp.log(row_total))[:, :, 0])

    starts = jnp.arange(row_count // block_rows, dtype=jnp.int32) * block_rows
    mixed_all, sums_all = lax.map(one_block, starts)
    head_count = queries.shape[1]
    attended = mixed_all.reshape(row_count, head_count, queries.shape[2])
    log_sums = jnp.transpose(sums_all, (1, 0, 2)).reshape(head_count, row_count)
    return (attended, log_sums)


def attend_back(queries, keys_b, values_b, log_sums, grad_attended, seq_ids, block_rows):
    row_count = keys_b.shape[0]
    head_dim = keys_b.shape[1]
    scaling = queries.shape[2] ** (-0.5)
    columns = jnp.arange(row_count, dtype=jnp.int32)

    def one_block(carried, row_start):
        keys_acc, values_acc = carried
        places = row_start + jnp.arange(block_rows, dtype=jnp.int32)
        allowed = (seq_ids[:, None] == seq_ids[None, :]) & (columns[None, :] <= places[:, None])
        scores = (
            jnp.einsum("ihd,jd->hij", queries, keys_b, preferred_element_type=jnp.float32) * scaling
        )
        scores = jnp.where(allowed[None], scores, -jnp.inf)
        probs_f = jnp.exp(scores - log_sums[:, :, None])
        grad_probs = jnp.einsum(
            "ihd,jd->hij", grad_attended, values_b, preferred_element_type=jnp.float32
        )
        grad_scores = probs_f * (grad_probs - jnp.sum(probs_f * grad_probs, axis=-1, keepdims=True))
        grad_scores_b = grad_scores.astype(jnp.bfloat16)
        grad_q = (
            jnp.einsum("hij,jd->ihd", grad_scores_b, keys_b, preferred_element_type=jnp.float32)
            * scaling
        )
        keys_acc = (
            keys_acc
            + jnp.einsum("hij,ihd->jd", grad_scores_b, queries, preferred_element_type=jnp.float32)
            * scaling
        )
        values_acc = values_acc + jnp.einsum(
            "hij,ihd->jd",
            probs_f.astype(jnp.bfloat16),
            grad_attended,
            preferred_element_type=jnp.float32,
        )
        return ((keys_acc, values_acc), grad_q)

    starts = jnp.arange(row_count // block_rows, dtype=jnp.int32) * block_rows
    zeros_kv = jnp.zeros((row_count, head_dim), jnp.float32)
    (grad_keys, grad_values), grad_q_all = lax.scan(one_block, (zeros_kv, zeros_kv), starts)
    return (grad_q_all.reshape(queries.shape), grad_keys, grad_values)


def send_ffn(grad_gate_up, grad_down):
    return (
        lax.psum_scatter(
            grad_gate_up.astype(jnp.bfloat16), "dp", scatter_dimension=0, tiled=True
        ).astype(jnp.float32),
        lax.psum_scatter(
            grad_down.astype(jnp.bfloat16), "dp", scatter_dimension=0, tiled=True
        ).astype(jnp.float32),
    )


def body(
    tokens,
    cotangent,
    seq_lengths,
    norm1_gain,
    norm2_gain,
    mixer_in,
    state_in,
    step_in,
    conv_inner,
    conv_state,
    step_bias,
    decay_log,
    skip_gain,
    mixer_out,
    query_in,
    key_value,
    attend_out,
    gate_up,
    down_out,
):
    share_rows = tokens.shape[0]
    model_width = tokens.shape[1]
    head_dim = HD
    row_start = lax.axis_index("tensor") * share_rows
    inputs = tokens.astype(jnp.float32)
    normed, norm1_back = jax.vjp(rms_scale, inputs, norm1_gain)
    normed_b = lax.all_gather(normed.astype(jnp.bfloat16), "tensor", axis=0, tiled=True)
    row_count = normed_b.shape[0]
    seq_ids, positions, is_live = segments(seq_lengths[0], row_count)
    live_share = lax.dynamic_slice_in_dim(is_live, row_start, share_rows, 0)[:, None]
    mixer_raw = product(normed_b, mixer_in.reshape(model_width, -1)).reshape(row_count, 2, -1)
    state_raw = product(normed_b, state_in)
    step_raw = product(normed_b, step_in)

    def mixer_local(
        gate_z, inner_x, state_part, step_part, conv_a, conv_b, bias_part, decay_part, skip_part
    ):
        return mamba_mixer(
            gate_z,
            inner_x,
            state_part,
            step_part,
            conv_a,
            conv_b,
            bias_part,
            decay_part,
            skip_part,
            seq_ids,
            SPAN,
        )

    gated, mixer_back = jax.vjp(
        mixer_local,
        mixer_raw[:, 0],
        mixer_raw[:, 1],
        state_raw,
        step_raw,
        conv_inner,
        conv_state,
        step_bias,
        decay_log,
        skip_gain,
    )
    gated_b = gated.astype(jnp.bfloat16)
    partial_sum = contract_last(gated_b, mixer_out)
    query_heads = query_in.shape[1] // head_dim
    key_index = lax.axis_index("tensor") * query_heads // (QH // KVH)
    pair_local = lax.dynamic_slice_in_dim(key_value, key_index * head_dim, head_dim, 2).reshape(
        model_width, 2 * head_dim
    )
    query_raw = product(normed_b, query_in).reshape(row_count, query_heads, head_dim)
    pair_raw = product(normed_b, pair_local).reshape(row_count, 2, head_dim)
    queries = rotate(query_raw, positions, 1.0).astype(jnp.bfloat16)
    keys_b = rotate(pair_raw[:, 0:1], positions, 1.0)[:, 0].astype(jnp.bfloat16)
    values_b = pair_raw[:, 1].astype(jnp.bfloat16)
    attended, log_sums = attend(queries, keys_b, values_b, seq_ids, ATT_ROWS)
    attended_b = attended.reshape(row_count, -1).astype(jnp.bfloat16)
    partial_sum = partial_sum + contract_last(attended_b, attend_out)
    hidden_in = inputs + lax.psum_scatter(partial_sum, "tensor", scatter_dimension=0, tiled=True)
    normed2, norm2_back = jax.vjp(rms_scale, hidden_in, norm2_gain)
    normed2_b = normed2.astype(jnp.bfloat16)
    ffn_rows = lax.all_gather(normed2_b, "tensor", axis=0, tiled=True)
    ffn_count = ffn_rows.shape[0]
    gate_raw = product(ffn_rows, gate_up.reshape(model_width, -1)).reshape(ffn_count, 2, -1)
    hidden_f, swiglu_back = jax.vjp(swiglu, gate_raw[:, 0], gate_raw[:, 1])
    hidden_b = hidden_f.astype(jnp.bfloat16)
    ffn_part = contract_last(hidden_b, down_out)
    ffn_share = lax.psum_scatter(
        ffn_part.astype(jnp.bfloat16), "tensor", scatter_dimension=0, tiled=True
    ).astype(jnp.float32)
    block_out = ((hidden_in + ffn_share) * live_share).astype(jnp.bfloat16)
    grad_out = cotangent.astype(jnp.float32) * live_share
    grad_out_b = grad_out.astype(jnp.bfloat16)
    grad_out_rows = lax.all_gather(grad_out_b, "tensor", axis=0, tiled=True)
    grad_hidden = product(grad_out_rows, down_out)
    grad_down = contract_first(grad_out_rows, hidden_b)
    grad_gate, grad_up = swiglu_back(grad_hidden)
    grad_gate_b = (
        jnp.stack([grad_gate, grad_up], axis=1).reshape(ffn_count, -1).astype(jnp.bfloat16)
    )
    grad_normed2 = contract_last(grad_gate_b, gate_up.reshape(model_width, -1))
    grad_gate_up = contract_first(ffn_rows, grad_gate_b).reshape(model_width, 2, -1)
    grad_normed2 = lax.psum_scatter(
        grad_normed2.astype(jnp.bfloat16), "tensor", scatter_dimension=0, tiled=True
    ).astype(jnp.float32)
    grad_hidden_in, grad_norm2 = norm2_back(grad_normed2)
    grad_hidden_in = grad_hidden_in + grad_out
    grad_mix_b = lax.all_gather(grad_hidden_in.astype(jnp.bfloat16), "tensor", axis=0, tiled=True)
    grad_gated = product(grad_mix_b, mixer_out)
    grad_mixer_out = contract_first(grad_mix_b, gated_b)
    grads_mixer = mixer_back(grad_gated)
    grad_zx_b = (
        jnp.stack([grads_mixer[0], grads_mixer[1]], axis=1)
        .reshape(row_count, -1)
        .astype(jnp.bfloat16)
    )
    grad_state_b = grads_mixer[2].astype(jnp.bfloat16)
    grad_step_b = grads_mixer[3].astype(jnp.bfloat16)
    grad_act = (
        contract_last(grad_zx_b, mixer_in.reshape(model_width, -1))
        + contract_last(grad_state_b, state_in)
        + contract_last(grad_step_b, step_in)
    )
    grad_mixer_in = contract_first(normed_b, grad_zx_b).reshape(model_width, 2, -1)
    grad_state_in = contract_first(normed_b, grad_state_b)
    grad_step_in = contract_first(normed_b, grad_step_b)
    grad_attended = (
        product(grad_mix_b, attend_out)
        .reshape(row_count, query_heads, head_dim)
        .astype(jnp.bfloat16)
    )
    grad_attend_out = contract_first(grad_mix_b, attended_b)
    grad_query, grad_keys, grad_values = attend_back(
        queries, keys_b, values_b, log_sums, grad_attended, seq_ids, ATT_ROWS
    )
    grad_query_b = rotate(grad_query, positions, -1.0).reshape(row_count, -1).astype(jnp.bfloat16)
    grad_pair_b = (
        jnp.stack([rotate(grad_keys[:, None], positions, -1.0)[:, 0], grad_values], axis=1)
        .reshape(row_count, -1)
        .astype(jnp.bfloat16)
    )
    grad_act = (
        grad_act + contract_last(grad_query_b, query_in) + contract_last(grad_pair_b, pair_local)
    )
    grad_query_in = contract_first(normed_b, grad_query_b)
    grad_pair = contract_first(normed_b, grad_pair_b).reshape(model_width, 2, head_dim)
    grad_key_value = lax.dynamic_update_slice_in_dim(
        jnp.zeros(key_value.shape, jnp.float32), grad_pair, key_index * head_dim, 2
    )
    grad_normed = lax.psum_scatter(
        grad_act.astype(jnp.bfloat16), "tensor", scatter_dimension=0, tiled=True
    ).astype(jnp.float32)
    grad_inputs, grad_norm1 = norm1_back(grad_normed)
    token_grad = (grad_hidden_in + grad_inputs).astype(jnp.bfloat16)
    grad_norm1, grad_norm2, grad_state_in, grad_key_value, grad_conv_state = (
        lax.psum(grad_norm1.astype(jnp.bfloat16), "tensor").astype(jnp.float32),
        lax.psum(grad_norm2.astype(jnp.bfloat16), "tensor").astype(jnp.float32),
        lax.psum(grad_state_in.astype(jnp.bfloat16), "tensor").astype(jnp.float32),
        lax.psum(grad_key_value.astype(jnp.bfloat16), "tensor").astype(jnp.float32),
        lax.psum(grads_mixer[5].astype(jnp.bfloat16), "tensor").astype(jnp.float32),
    )
    minor_totals = lax.psum(
        (
            grad_norm1,
            grad_norm2,
            grads_mixer[4],
            grad_conv_state,
            grads_mixer[6],
            grads_mixer[7],
            grads_mixer[8],
        ),
        "dp",
    )
    ffn_grads = send_ffn(grad_gate_up, grad_down)
    bulk_totals = (
        lax.psum_scatter(
            grad_mixer_in.astype(jnp.bfloat16), "dp", scatter_dimension=0, tiled=True
        ).astype(jnp.float32),
        lax.psum_scatter(
            grad_state_in.astype(jnp.bfloat16), "dp", scatter_dimension=0, tiled=True
        ).astype(jnp.float32),
        lax.psum_scatter(
            grad_step_in.astype(jnp.bfloat16), "dp", scatter_dimension=0, tiled=True
        ).astype(jnp.float32),
        lax.psum_scatter(
            grad_mixer_out.astype(jnp.bfloat16), "dp", scatter_dimension=0, tiled=True
        ).astype(jnp.float32),
        lax.psum_scatter(
            grad_query_in.astype(jnp.bfloat16), "dp", scatter_dimension=0, tiled=True
        ).astype(jnp.float32),
        lax.psum_scatter(
            grad_key_value.astype(jnp.bfloat16), "dp", scatter_dimension=0, tiled=True
        ).astype(jnp.float32),
        lax.psum_scatter(
            grad_attend_out.astype(jnp.bfloat16), "dp", scatter_dimension=0, tiled=True
        ).astype(jnp.float32),
    )
    return (
        block_out,
        token_grad,
        minor_totals[0],
        minor_totals[1],
        bulk_totals[0],
        bulk_totals[1],
        bulk_totals[2],
        minor_totals[2],
        minor_totals[3],
        minor_totals[4],
        minor_totals[5],
        minor_totals[6],
        bulk_totals[3],
        bulk_totals[4],
        bulk_totals[5],
        bulk_totals[6],
        ffn_grads[0],
        ffn_grads[1],
    )


def solution(mesh):
    return jax.shard_map(
        body,
        mesh=mesh,
        in_specs=(
            P(("dp", "tensor"), None),
            P(("dp", "tensor"), None),
            P("dp", None),
            P(),
            P(),
            P(None, None, "tensor"),
            P(),
            P(None, "tensor"),
            P(None, "tensor"),
            P(),
            P("tensor"),
            P("tensor"),
            P("tensor"),
            P(None, "tensor"),
            P(None, "tensor"),
            P(),
            P(None, "tensor"),
            P(None, None, "tensor"),
            P(None, "tensor"),
        ),
        out_specs=(
            P(("dp", "tensor"), None),
            P(("dp", "tensor"), None),
            P(),
            P(),
            P("dp", None, "tensor"),
            P("dp", None),
            P("dp", "tensor"),
            P(None, "tensor"),
            P(),
            P("tensor"),
            P("tensor"),
            P("tensor"),
            P("dp", "tensor"),
            P("dp", "tensor"),
            P("dp", None, None),
            P("dp", "tensor"),
            P("dp", None, "tensor"),
            P("dp", "tensor"),
        ),
        check_vma=False,
    )
```

profile of v0, /device:TPU:0, one launch (start us, length us, event | category | flops | bytes accessed | tf_op | source)
XLA Modules:
  0.0 1226.2 jit_solution(7543779060406063926)
XLA Ops:
  16.0 12.9 %all_gather.12 = bf16[384,1024]{1,0:T(8,128)(2,1)S(1)} all-gather(bf16[192,1024]{1,0:T(8,128)(2,1)S(1)} %fusion.134), channel_id=1, replica_groups=mesh['dp'=16,'tensor'=2] {'tensor'}, dimensions={0}, use_global_device_ids=true | all-gather | bytes 1179648 | tf_op jit(solution)/shard_map/all_gather | solution.py:273
  37.7 5.2 copy.163
  63.7 49.4 %while.52 = (s32[]{:T(128)}, f32[12,64,128]{2,1,0:T(8,128)S(1)}, f32[3,128,12,64]{1,3,2,0:T(8,128)}, f32[3,12,64,128]{3,2,1,0:T(8,128)}, f32[3,128,12]{2,1,0:T(8...) while((s32[]{:T(128)}, f32[12,64,128]{2,1,0:T(8,128)S(1)}, ...), condition=%wide.region_5.6_spmd.clone, body=%wide.region_3.5_spmd.clone.sunk | while | flops 479977472 | bytes 4508627 | solution.py:102
  72.7 3.5 fusion.317
  89.2 3.6 fusion.317
  105.6 3.6 fusion.317
  127.7 5.6 copy.207
  133.3 6.7 copy.171
  141.9 19.5 %all_gather.14 = bf16[384,1024]{1,0:T(8,128)(2,1)} all-gather(bf16[192,1024]{1,0:T(8,128)(2,1)S(1)} %fusion.153), channel_id=1, replica_groups=mesh['dp'=16,'tensor'=2] {'tensor'}, dimensions={0}, use_global_device_ids=true | all-gather | bytes 1179648 | tf_op jit(solution)/shard_map/all_gather | solution.py:340
  163.8 11.2 all_gather.13
  184.7 17.2 %reduce-scatter.19.cloned.1.call-done = bf16[192,1024]{1,0:T(8,128)(2,1)} async-done(((bf16[384,1024]{1,0:T(8,128)(2,1)}), bf16[192,1024]{1,0:T(8,128)(2,1)}) %reduce-scatter.19.cloned.1.call-update) | async-done | bytes 393232 | tf_op jit(solution)/shard_map/reduce_scatter | solution.py:349
  205.5 11.5 all_gather.15
  217.1 4.4 multiply_reduce_fusion.5
  239.5 130.2 %while.53 = (s32[]{:T(128)}, f32[12]{0:T(128)}, f32[12,64,128]{2,1,0:T(8,128)}, f32[3,128,12,64]{1,3,2,0:T(8,128)}, f32[3,128,12]{2,1,0:T(8,128)}, /*index=5*/f3...) while((s32[]{:T(128)}, f32[12]{0:T(128)}, ...), condition=%wide.region_26.27_spmd.clone, body=%wide.region_14.26_spmd.clone.sunk | while | flops 1137679872 | bytes 13746742 | solution.py:102
  262.4 3.5 fusion.338
  306.1 3.5 fusion.338
  376.3 4.5 multiply_reduce_fusion.8
  386.2 31.6 %dynamic_update_slice.61 = bf16[1024,2,128]{2,1,0:T(2,128)(2,1)} dynamic-update-slice(bf16[1024,2,128]{2,1,0:T(2,128)(2,1)} %broadcast_in_dim.337, bf16[1024,2,64]{2,1,0:T(2,128)(2,1)} %copy.185, s32[]{:T(128)} %constant.218.clone.1, s32[]{:T(128)} %constant.218.clone.1, s32[]{:T(128)S(6)} %select_n.113) | dynamic-update-slice | bytes 524292 | tf_op jit(solution)/shard_map/dynamic_update_slice | solution.py:393
  450.7 195.1 %all-reduce.33.cloned.1.call-done = bf16[1024,2,128]{2,1,0:T(2,128)(2,1)} async-done(((bf16[1024,2,128]{2,1,0:T(2,128)(2,1)}), bf16[1024,2,128]{2,1,0:T(2,128)(2,1)}) %all-reduce.33.cloned.1.call-update) | async-done | bytes 524304
  647.2 18.7 %reduce-scatter.21.cloned.1.call-done = bf16[192,1024]{1,0:T(8,128)(2,1)} async-done(((bf16[384,1024]{1,0:T(8,128)(2,1)}), bf16[192,1024]{1,0:T(8,128)(2,1)}) %reduce-scatter.21.cloned.1.call-update) | async-done | bytes 393232 | tf_op jit(solution)/shard_map/reduce_scatter | solution.py:396
  667.8 58.3 %reduce-scatter.35.cloned.1.call-done = bf16[64,256]{1,0:T(8,128)(2,1)} async-done(((bf16[1024,256]{1,0:T(8,128)(2,1)}), bf16[64,256]{1,0:T(8,128)(2,1)}) %reduce-scatter.35.cloned.1.call-update) | async-done | bytes 32784 | tf_op jit(solution)/shard_map/reduce_scatter | solution.py:425
  735.1 6.1 convolution_convert_fusion
  746.1 4.8 convolution_convert_fusion.1
  751.9 32.5 %reduce-scatter.37.cloned.1.call-done = bf16[64,12]{1,0:T(8,128)(2,1)} async-done(((bf16[1024,12]{1,0:T(8,128)(2,1)}), bf16[64,12]{1,0:T(8,128)(2,1)}) %reduce-scatter.37.cloned.1.call-update) | async-done | bytes 1552
  785.8 57.0 %reduce-scatter.27.cloned.1.call-done = bf16[64,256]{1,0:T(8,128)(2,1)} async-done(((bf16[1024,256]{1,0:T(8,128)(2,1)}), bf16[64,256]{1,0:T(8,128)(2,1)}) %reduce-scatter.27.cloned.1.call-update) | async-done | bytes 32784 | tf_op jit(solution)/shard_map/reduce_scatter | solution.py:434
  844.2 57.4 %reduce-scatter.29.cloned.1.call-done = bf16[64,256]{1,0:T(8,128)(2,1)} async-done(((bf16[1024,256]{1,0:T(8,128)(2,1)}), bf16[64,256]{1,0:T(8,128)(2,1)}) %reduce-scatter.29.cloned.1.call-update) | async-done | bytes 32784 | tf_op jit(solution)/shard_map/reduce_scatter | solution.py:440
  903.0 63.0 %reduce-scatter.33.cloned.1.call-done = bf16[64,1024]{1,0:T(8,128)(2,1)} async-done(((bf16[1024,1024]{1,0:T(8,128)(2,1)}), bf16[64,1024]{1,0:T(8,128)(2,1)}) %reduce-scatter.33.cloned.1.call-update) | async-done | bytes 131088 | tf_op jit(solution)/shard_map/reduce_scatter | solution.py:240
  967.6 17.0 %reduce-scatter.17.cloned.1.call-done = bf16[192,1024]{1,0:T(8,128)(2,1)} async-done(((bf16[384,1024]{1,0:T(8,128)(2,1)}), bf16[192,1024]{1,0:T(8,128)(2,1)}) %reduce-scatter.17.cloned.1.call-update) | async-done | bytes 393232 | tf_op jit(solution)/shard_map/reduce_scatter | solution.py:334
  987.4 21.6 %all-reduce.35.cloned.1.call-done = (bf16[1024]{0:T(1024)(128)(2,1)}, bf16[1024]{0:T(1024)(128)(2,1)}, bf16[4,256]{1,0:T(4,128)(2,1)}, bf16[64,256]{1,0:T(8,128)(2,1)}, bf16[64,2,128]{2,1,0:T(2,128)(2,1)}) async-done(((bf16[1024]{0:T(1024)(128)(2,1)}, bf16[1024]{0:T(1024)(128)(2,1)}, bf16[4,256]{1,0:T(4,128)(2,1)}, bf16[64,256]{1,0:T(8,128)(2,1)}, bf16[64,2,128]{2,1,0:T(2,128)(2,1)}), ...) | async-done | bytes 71696 | tf_op jit(solution)/shard_map/psum | solution.py:402
  1011.8 60.8 %all-reduce.28 = (f32[1024]{0:T(1024)}, f32[1024]{0:T(1024)}, f32[4,768]{1,0:T(4,128)}, f32[4,256]{1,0:T(4,128)}, f32[12]{0:T(128)}, /*index=5*/f32[12]{0:T(128)}, f32[12]{0:T(128)}) all-reduce(bf16[1024]{0:T(1024)(128)(2,1)} %get-tuple-element.897, ...), channel_id=1, replica_groups=mesh['dp'=16,'tensor'=2] {'dp'}, use_global_device_ids=true, to_apply=%region_32.33 | all-reduce | flops 6180 | bytes 43296 | tf_op jit(solution)/shard_map/psum | solution.py:408
  1074.5 74.2 %reduce-scatter.31.cloned.1.call-done = bf16[64,2,1024]{2,0,1:T(8,128)(2,1)} async-done(((bf16[1024,2,1024]{2,0,1:T(8,128)(2,1)}), bf16[64,2,1024]{2,0,1:T(8,128)(2,1)}) %reduce-scatter.31.cloned.1.call-update) | async-done | bytes 262160 | tf_op jit(solution)/shard_map/reduce_scatter | solution.py:237
  1150.6 67.0 %reduce-scatter.23.cloned.1.call-done = bf16[64,2,768]{2,0,1:T(8,128)(2,1)} async-done(((bf16[1024,2,768]{2,0,1:T(8,128)(2,1)}), bf16[64,2,768]{2,0,1:T(8,128)(2,1)}) %reduce-scatter.23.cloned.1.call-update) | async-done | bytes 196624 | tf_op jit(solution)/shard_map/reduce_scatter | solution.py:422
  (711 shorter events, 320.2 us)
Async XLA Ops:
  7.2 170.5 %copy-start = (bf16[1024,1024]{1,0:T(8,128)(2,1)S(1)}, bf16[1024,1024]{1,0:T(8,128)(2,1)}, u32[]{:S(2)}) copy-start(bf16[1024,1024]{1,0:T(8,128)(2,1)} %param.41) | copy-start | bytes 6291460
  7.2 154.9 %reduce-scatter.15.cloned.1.call-start = ((), (), s32[]{:S(2)}) async-start(), calls=%async_computation.12 | async-start | bytes 2359296 | tf_op jit(solution)/shard_map/reduce_scatter | solution.py:325
  10.8 46.8 %copy-start.103 = (pred[384]{0:T(512)(128)(4,1)}, pred[384]{0:T(512)(128)(4,1)S(1)}, u32[]{:S(2)}) copy-start(pred[384]{0:T(512)(128)(4,1)S(1)} %get-tuple-element.960) | copy-start | bytes 1156
  10.8 46.8 %copy-start.105 = (pred[384]{0:T(512)(128)(4,1)}, pred[384]{0:T(512)(128)(4,1)S(1)}, u32[]{:S(2)}) copy-start(pred[384]{0:T(512)(128)(4,1)S(1)} %get-tuple-element.961) | copy-start | bytes 1156
  28.9 197.8 %copy-start.1 = (bf16[384,1024]{1,0:T(8,128)(2,1)}, bf16[384,1024]{1,0:T(8,128)(2,1)S(1)}, u32[]{:S(2)}) copy-start(bf16[384,1024]{1,0:T(8,128)(2,1)S(1)} %all_gather.12) | copy-start | bytes 2359300
  119.8 109.5 %copy-start.85 = (f32[768]{0:T(1024)}, f32[768]{0:T(1024)S(1)}, u32[]{:S(2)}) copy-start(f32[768]{0:T(1024)S(1)} %mul.1174) | copy-start | bytes 9220
  126.5 75.4 %reduce-scatter.19.cloned.1.call-start = ((), (), s32[]{:S(2)}) async-start(), calls=%async_computation.14 | async-start | bytes 1179648 | tf_op jit(solution)/shard_map/reduce_scatter | solution.py:349
  140.8 63.3 %copy-start.119 = (f32[192]{0:T(256)}, f32[192]{0:T(256)S(1)}, u32[]{:S(2)}) copy-start(f32[192]{0:T(256)S(1)} %dynamic_slice.120) | copy-start | bytes 2308
  163.6 40.5 %copy-start.101 = (f32[192]{0:T(256)}, f32[192]{0:T(256)S(1)}, u32[]{:S(2)}) copy-start(f32[192]{0:T(256)S(1)} %fusion.194) | copy-start | bytes 2308
  184.5 461.2 %all-reduce.33.cloned.1.call-start = ((), (), s32[]{:S(2)}) async-start(), calls=%async_computation.24 | async-start | bytes 1048576
  385.1 32.8 %copy-start.51 = (f32[3,128,128]{2,1,0:T(8,128)S(1)}, f32[3,128,128]{2,1,0:T(8,128)}, u32[]{:S(2)}) copy-start(f32[3,128,128]{2,1,0:T(8,128)} %get-tuple-element.529) | copy-start | bytes 589828
  417.9 248.0 %reduce-scatter.21.cloned.1.call-start = ((), (), s32[]{:S(2)}) async-start(), calls=%async_computation.15 | async-start | bytes 1179648 | tf_op jit(solution)/shard_map/reduce_scatter | solution.py:396
  433.1 293.0 %reduce-scatter.35.cloned.1.call-start = ((), (), s32[]{:S(2)}) async-start(), calls=%async_computation.22 | async-start | bytes 557056 | tf_op jit(solution)/shard_map/reduce_scatter | solution.py:425
  434.4 349.9 %reduce-scatter.37.cloned.1.call-start = ((), (), s32[]{:S(2)}) async-start(), calls=%async_computation.23 | async-start | bytes 278528
  435.6 407.2 %reduce-scatter.27.cloned.1.call-start = ((), (), s32[]{:S(2)}) async-start(), calls=%async_computation.18 | async-start | bytes 557056 | tf_op jit(solution)/shard_map/reduce_scatter | solution.py:434
  436.9 464.6 %reduce-scatter.29.cloned.1.call-start = ((), (), s32[]{:S(2)}) async-start(), calls=%async_computation.19 | async-start | bytes 557056 | tf_op jit(solution)/shard_map/reduce_scatter | solution.py:440
  439.4 526.5 %reduce-scatter.33.cloned.1.call-start = ((), (), s32[]{:S(2)}) async-start(), calls=%async_computation.21 | async-start | bytes 2228224 | tf_op jit(solution)/shard_map/reduce_scatter | solution.py:240
  445.6 220.3 %copy-start.21 = (bf16[192,1024]{1,0:T(8,128)(2,1)S(1)}, bf16[192,1024]{1,0:T(8,128)(2,1)}, u32[]{:S(2)}) copy-start(bf16[192,1024]{1,0:T(8,128)(2,1)} %param.23) | copy-start | bytes 1179652
  445.6 220.3 %copy-start.90 = (f32[1024]{0:T(1024)S(1)}, f32[1024]{0:T(1024)}, u32[]{:S(2)}) copy-start(f32[1024]{0:T(1024)} %param.26) | copy-start | bytes 12292
  445.6 220.3 %copy-start.118 = (f32[192]{0:T(256)S(1)}, f32[192]{0:T(256)}, u32[]{:S(2)}) copy-start(f32[192]{0:T(256)} %copy-done.117) | copy-start | bytes 2308
  445.6 539.0 %reduce-scatter.17.cloned.1.call-start = ((), (), s32[]{:S(2)}) async-start(), calls=%async_computation.13 | async-start | bytes 1179648 | tf_op jit(solution)/shard_map/reduce_scatter | solution.py:334
  448.7 560.2 %all-reduce.35.cloned.1.call-start = ((), (), s32[]{:S(2)}) async-start(), calls=%async_computation.25 | async-start | bytes 143360 | tf_op jit(solution)/shard_map/psum | solution.py:402
  726.0 346.8 %reduce-scatter.25.cloned.1.call-start = ((), (), s32[]{:S(2)}) async-start(), calls=%async_computation.17 | async-start | bytes 1671168 | tf_op jit(solution)/shard_map/reduce_scatter | solution.py:431
  729.6 419.0 %reduce-scatter.31.cloned.1.call-start = ((), (), s32[]{:S(2)}) async-start(), calls=%async_computation.20 | async-start | bytes 4456448 | tf_op jit(solution)/shard_map/reduce_scatter | solution.py:237
  741.2 476.4 %reduce-scatter.23.cloned.1.call-start = ((), (), s32[]{:S(2)}) async-start(), calls=%async_computation.16 | async-start | bytes 3342336 | tf_op jit(solution)/shard_map/reduce_scatter | solution.py:422
  750.9 216.7 %copy-start.132 = (f32[192]{0:T(256)S(1)}, f32[192]{0:T(256)}, u32[]{:S(2)}) copy-start(f32[192]{0:T(256)} %copy-done.131) | copy-start | bytes 2308
  750.9 233.7 %copy-start.9 = (f32[192,1024]{1,0:T(8,128)S(1)}, f32[192,1024]{1,0:T(8,128)}, u32[]{:S(2)}) copy-start(f32[192,1024]{1,0:T(8,128)} %copy-done.7) | copy-start | bytes 2359300
  750.9 233.7 %copy-start.88 = (f32[1024]{0:T(1024)S(1)}, f32[1024]{0:T(1024)}, u32[]{:S(2)}) copy-start(f32[1024]{0:T(1024)} %param.27) | copy-start | bytes 12292
  750.9 233.7 %copy-start.102 = (f32[192]{0:T(256)S(1)}, f32[192]{0:T(256)}, u32[]{:S(2)}) copy-start(f32[192]{0:T(256)} %copy-done.101) | copy-start | bytes 2308
  750.9 233.6 %copy-start.120 = (f32[192]{0:T(256)S(1)}, f32[192]{0:T(256)}, u32[]{:S(2)}) copy-start(f32[192]{0:T(256)} %copy-done.119) | copy-start | bytes 2308
  751.0 233.6 %copy-start.128 = (f32[192]{0:T(256)S(1)}, f32[192]{0:T(256)}, u32[]{:S(2)}) copy-start(f32[192]{0:T(256)} %copy-done.127) | copy-start | bytes 2308
  967.6 44.2 %copy-start.148 = (f32[12]{0:T(128)S(1)}, f32[12]{0:T(128)}, u32[]{:S(2)}) copy-start(f32[12]{0:T(128)} %get-tuple-element.908) | copy-start | bytes 148
  (168 other events, 563.0 us)
Sparse Core Ops, SparseCore 0:
  126.6 35.4 reduce-scatter.14
  184.7 17.1 reduce-scatter.18
  418.0 227.7 all-reduce.32
  647.9 17.9 reduce-scatter.20
  670.2 55.7 reduce-scatter.34
  730.0 54.3 reduce-scatter.36
  787.9 54.8 reduce-scatter.26
  846.7 54.7 reduce-scatter.28
  905.3 60.5 reduce-scatter.32
  968.1 16.4 reduce-scatter.16
  988.3 20.6 all-reduce.34
  1012.5 60.3 reduce-scatter.24
  1077.2 71.3 reduce-scatter.30
  1152.3 65.2 reduce-scatter.22
where the time goes:
time: 1230 us
  waiting for transfers between devices  680 us (55%)
  local copies, waits for them, and re-layouts  163 us (13%)
  matrix products  137 us (11%)
  blocking collectives  116 us (9%)
  other arithmetic  105 us (9%)
  between operations  16.2 us (1%)
    unnamed x16, waiting for transfers between devices  228 us
    reduce_scatter x1, waiting for transfers between devices, send_ffn(): lax.psum_scatter(grad_gate_up.astype(jnp.bfloat16), 'dp', scatter_dimensi...  74.2 us
    reduce_scatter x1, waiting for transfers between devices, body(): lax.psum_scatter(grad_mixer_in.astype(jnp.bfloat16), 'dp', scatter_dimens...  67 us
    reduce_scatter x1, waiting for transfers between devices, send_ffn(): lax.psum_scatter(grad_down.astype(jnp.bfloat16), 'dp', scatter_dimension=...  63 us
    psum x1, blocking collectives, body(): lax.psum((grad_norm1, grad_norm2, grads_mixer[4], grad_conv_state, grads_...  60.8 us
    reduce_scatter x1, waiting for transfers between devices, body(): lax.psum_scatter(grad_state_in.astype(jnp.bfloat16), 'dp', scatter_dimens...  58.3 us
    reduce_scatter x1, waiting for transfers between devices, body(): lax.psum_scatter(grad_attend_out.astype(jnp.bfloat16), 'dp', scatter_dime...  57.4 us
    reduce_scatter x1, waiting for transfers between devices, body(): lax.psum_scatter(grad_query_in.astype(jnp.bfloat16), 'dp', scatter_dimens...  57 us
  transfers between devices with their start and end apart: 14, of which 14 were waited for; matrix products, arithmetic and copies ran while one was open for 7% of the time, Pallas kernels for 0%

commit v1 on v0

v1 whole, which is shorter than its diff:
```python
import functools

import jax
import jax.numpy as jnp
from jax import lax
from jax.experimental import pallas as pl
from jax.experimental.pallas import tpu as pltpu
from jax.sharding import PartitionSpec as P

HD = 64
QH = 8
KVH = 2
LANES = 128

rope_base = 100000000000.0
norm_eps = 1e-05
far = -1e30
highest = lax.Precision.HIGHEST
f32 = jnp.float32
bf16 = jnp.bfloat16


def padded(width):
    return -(-width // LANES) * LANES


def pad_to(values, width):
    return jnp.pad(values, [(0, 0)] * (values.ndim - 1) + [(0, width - values.shape[-1])])


def mm(left, right):
    return jnp.dot(left, right, preferred_element_type=f32)


def mm_nt(left, right):
    return lax.dot_general(left, right, (((1,), (1,)), ((), ())), preferred_element_type=f32)


def mm_tn(left, right):
    return lax.dot_general(left, right, (((0,), (0,)), ((), ())), preferred_element_type=f32)


def mm_exact(left, right):
    return jnp.dot(left, right, preferred_element_type=f32, precision=highest)


def lane_ids(rows):
    return lax.broadcasted_iota(jnp.int32, (rows, LANES), 1)


def partner_half(values):
    lane = lane_ids(values.shape[0])
    return jnp.where(lane % HD < HD // 2, pltpu.roll(values, LANES - HD // 2, 1), pltpu.roll(values, HD // 2, 1))


def rotated(values, cosine, signed_sine):
    return values * cosine + partner_half(values) * signed_sine


def conv_terms(values, masks):
    return [pltpu.roll(values, offset, 0) * masks[offset] for offset in (3, 2, 1)] + [values]


def conv_back(grad, masks, taps):
    rows = grad.shape[0]
    total = grad * taps[3:4]
    for offset in (1, 2, 3):
        total = total + pltpu.roll(grad * masks[offset], rows - offset, 0) * taps[3 - offset : 4 - offset]
    return total


def link_bias(seq_col, seq_row, transposed):
    rows = seq_col.shape[0]
    down = lax.broadcasted_iota(jnp.int32, (rows, rows), 0)
    across = lax.broadcasted_iota(jnp.int32, (rows, rows), 1)
    ordered = down <= across if transposed else down >= across
    return (seq_col == seq_row) & ordered


def step_parts(raw, bias):
    shifted = raw + bias
    return jnp.maximum(shifted, 0.0) + jnp.log1p(jnp.exp(-jnp.abs(shifted)))


def spread_heads(columns, first, width):
    rows = columns.shape[0]
    low = jnp.broadcast_to(columns[:, first : first + 1], (rows, LANES))
    if width <= HD:
        return low
    high = jnp.broadcast_to(columns[:, first + 1 : first + 2], (rows, LANES))
    return jnp.where(lane_ids(rows) < HD, low, high)


def half_mask(rows, side):
    lane = lane_ids(rows)
    return lane < HD if side == 0 else lane >= HD


def front_kernel(
    dims, x_ref, gain_ref, wcat_ref, wout_ref, seqc_ref, seqr_ref, masks_ref, cos_ref, sin_ref,
    convx_ref, convs_ref, bias_ref, rate_ref, skip_ref,
    act_ref, proj_ref, scan_ref, cat_ref, part_ref, neg_ref, g_ref, xdt_ref,
):
    heads, qheads, wp, qwp, span = dims
    rows = x_ref.shape[0]
    x = x_ref[...].astype(f32)
    act = (x * lax.rsqrt(jnp.mean(x * x, axis=-1, keepdims=True) + norm_eps) * gain_ref[...]).astype(bf16)
    act_ref[...] = act
    proj_ref[...] = mm(act, wcat_ref[...])
    at_state, at_step, at_query, at_pair = 2 * wp, 2 * wp + 256, 2 * wp + 384, 2 * wp + 384 + qwp
    masks = {k: masks_ref[:, k : k + 1] for k in (1, 2, 3)}
    linked = link_bias(seqc_ref[...], seqr_ref[...], False)
    neg_ref[...] = jnp.where(linked, 0.0, far)
    dt = step_parts(proj_ref[:, at_step : at_step + LANES], bias_ref[...])
    decay = mm_exact(jnp.where(linked, 1.0, 0.0), -dt * rate_ref[...])
    decay_t = decay.T
    state = proj_ref[:, at_state : at_state + 256]
    terms = conv_terms(state, masks)
    bcc = sum(t * convs_ref[k : k + 1, :] for k, t in enumerate(terms))
    bcc = (bcc * jax.nn.sigmoid(bcc)).astype(bf16)
    g_ref[...] = mm_nt(bcc[:, 128:], bcc[:, :128])

    for p in range(wp // LANES):
        cols = slice(p * LANES, (p + 1) * LANES)
        width = HD * min(2, heads - 2 * p)
        raw = proj_ref[:, wp + p * LANES : wp + (p + 1) * LANES]
        conv = sum(t * convx_ref[k : k + 1, cols] for k, t in enumerate(conv_terms(raw, masks)))
        xc = conv * jax.nn.sigmoid(conv)
        xdt_ref[...] = (xc * spread_heads(dt, 2 * p, width)).astype(bf16)
        blocks = []
        for a in range(rows // span):
            here = slice(a * span, (a + 1) * span)
            reach = (a + 1) * span
            sides = []
            for h in range(2 * p, 2 * p + width // HD):
                gap = decay[here, h : h + 1] - decay_t[h : h + 1, :reach]
                mixing = g_ref[here, :reach] * jnp.exp(gap + neg_ref[here, :reach])
                sides.append(mm(mixing.astype(bf16), xdt_ref[:reach, :]))
            blocks.append(sides[0] if len(sides) == 1 else jnp.where(half_mask(span, 0), sides[0], sides[1]))
        scanned = jnp.concatenate(blocks, axis=0)
        scan_ref[:, cols] = scanned
        z = proj_ref[:, cols]
        cat_ref[:, cols] = ((scanned + skip_ref[:, cols] * xc) * (z * jax.nn.sigmoid(z))).astype(bf16)

    cosine, sine = cos_ref[...], sin_ref[...]
    pair = proj_ref[:, at_pair : at_pair + LANES]
    swapped = pltpu.roll(pair, HD, 1)
    lower = half_mask(rows, 0)
    keys = rotated(jnp.where(lower, pair, swapped), cosine, sine).astype(bf16)
    values = jnp.where(lower, swapped, pair).astype(bf16)
    for p in range(qwp // LANES):
        cols = slice(wp + p * LANES, wp + (p + 1) * LANES)
        queries = rotated(proj_ref[:, at_query + p * LANES : at_query + (p + 1) * LANES], cosine, sine).astype(bf16)
        for a in range(rows // span):
            here = slice(a * span, (a + 1) * span)
            reach = (a + 1) * span
            sides = []
            for side in range(min(2, qheads - 2 * p)):
                q = jnp.where(half_mask(span, side), queries[here], jnp.zeros((), bf16))
                scores = mm_nt(q, keys[:reach]) * (HD**-0.5) + neg_ref[here, :reach]
                weights = jnp.exp(scores - jnp.max(scores, axis=-1, keepdims=True))
                probs = weights / jnp.sum(weights, axis=-1, keepdims=True)
                sides.append(mm(probs.astype(bf16), values[:reach]))
            if len(sides) == 1:
                out = jnp.where(half_mask(span, 0), sides[0], 0.0)
            else:
                out = jnp.where(half_mask(span, 0), sides[0], sides[1])
            cat_ref[here, cols] = out.astype(bf16)
    part_ref[...] = mm_nt(cat_ref[...], wout_ref[...]).astype(bf16)


def middle_kernel(
    x_ref, own_ref, other_ref, gain_ref, wgu_ref, down_ref, dhid_ref,
    h1_ref, n2_ref, hidden_ref, dgu_ref, out_ref, dn2_ref,
):
    width = down_ref.shape[1]
    h1 = x_ref[...].astype(f32) + (own_ref[...].astype(f32) + other_ref[...].astype(f32))
    h1_ref[...] = h1
    n2 = (h1 * lax.rsqrt(jnp.mean(h1 * h1, axis=-1, keepdims=True) + norm_eps) * gain_ref[...]).astype(bf16)
    n2_ref[...] = n2
    gate = mm(n2, wgu_ref[:, :width])
    up = mm(n2, wgu_ref[:, width:])
    sig = jax.nn.sigmoid(gate)
    silu = gate * sig
    hidden = (silu * up).astype(bf16)
    hidden_ref[...] = hidden
    dhid = dhid_ref[...].astype(f32)
    dgu_ref[:, :width] = (dhid * up * (sig * (1.0 + gate * (1.0 - sig)))).astype(bf16)
    dgu_ref[:, width:] = (dhid * silu).astype(bf16)
    dn2_ref[...] = mm_nt(dgu_ref[...], wgu_ref[...]).astype(bf16)
    out_ref[...] = mm_nt(hidden, down_ref[...]).astype(bf16)


def back_kernel(
    dims, own_ref, other_ref, h1_ref, dout_ref, gain2_ref, x_ref, wcat_ref, wout_ref, seqc_ref, seqr_ref, masks_ref,
    cos_ref, sin_ref, convx_ref, convs_ref, bias_ref, rate_ref, skip_ref, proj_ref, scan_ref,
    dh1_ref, dmix_ref, dall_ref, dact_ref, gn1_ref, gn2_ref, gcx_ref, gcs_ref, gstep_ref, gskip_ref,
    neg_ref, gt_ref, dgt_ref, dcat_ref, dsum_ref, ddir_ref, dk_ref, dv_ref,
):
    heads, qheads, wp, qwp, span = dims
    rows = x_ref.shape[0]
    at_state, at_step, at_query, at_pair = 2 * wp, 2 * wp + 256, 2 * wp + 384, 2 * wp + 384 + qwp
    dn2 = own_ref[...].astype(f32) + other_ref[...].astype(f32)
    h1 = h1_ref[...]
    r2 = lax.rsqrt(jnp.mean(h1 * h1, axis=-1, keepdims=True) + norm_eps)
    u = dn2 * gain2_ref[...]
    dh1 = dout_ref[...].astype(f32) + r2 * u - h1 * (r2 * r2 * r2 * jnp.mean(u * h1, axis=-1, keepdims=True))
    gn2_ref[...] = jnp.sum(dn2 * h1 * r2, axis=0, keepdims=True)
    dh1_ref[...] = dh1
    dmix = dh1.astype(bf16)
    dmix_ref[...] = dmix
    dcat_ref[...] = mm(dmix, wout_ref[...])

    masks = {k: masks_ref[:, k : k + 1] for k in (1, 2, 3)}
    linked_t = link_bias(seqc_ref[...], seqr_ref[...], True)
    neg_ref[...] = jnp.where(linked_t, 0.0, far)
    lower = half_mask(rows, 0)
    cosine, sine = cos_ref[...], sin_ref[...]
    pair = proj_ref[:, at_pair : at_pair + LANES]
    swapped = pltpu.roll(pair, HD, 1)
    keys = rotated(jnp.where(lower, pair, swapped), cosine, sine).astype(bf16)
    values = jnp.where(lower, swapped, pair).astype(bf16)
    dk_ref[...] = jnp.zeros_like(dk_ref)
    dv_ref[...] = jnp.zeros_like(dv_ref)
    for p in range(qwp // LANES):
        at = at_query + p * LANES
        queries = rotated(proj_ref[:, at : at + LANES], cosine, sine).astype(bf16)
        datt = dcat_ref[:, wp + p * LANES : wp + (p + 1) * LANES].astype(bf16)
        blocks = []
        for a in range(rows // span):
            here = slice(a * span, (a + 1) * span)
            reach = (a + 1) * span
            sides = []
            for side in range(min(2, qheads - 2 * p)):
                half = half_mask(span, side)
                q = jnp.where(half, queries[here], jnp.zeros((), bf16))
                do = jnp.where(half, datt[here], jnp.zeros((), bf16))
                scores = mm_nt(keys[:reach], q) * (HD**-0.5) + neg_ref[:reach, here]
                weights = jnp.exp(scores - jnp.max(scores, axis=0, keepdims=True))
                probs = weights / jnp.sum(weights, axis=0, keepdims=True)
                dp = mm_nt(values[:reach], do)
                ds = (probs * (dp - jnp.sum(probs * dp, axis=0, keepdims=True))).astype(bf16)
                dk_ref[:reach, :] += mm(ds, q)
                dv_ref[:reach, :] += mm(probs.astype(bf16), do)
                sides.append(mm_tn(ds, keys[:reach]))
            if len(sides) == 1:
                blocks.append(jnp.where(half_mask(span, 0), sides[0], 0.0))
            else:
                blocks.append(jnp.where(half_mask(span, 0), sides[0], sides[1]))
        dq = jnp.concatenate(blocks, axis=0) * (HD**-0.5)
        dall_ref[:, at : at + LANES] = rotated(dq, cosine, -sine).astype(bf16)
    dk = dk_ref[...] * (HD**-0.5)
    dk = rotated(dk + pltpu.roll(dk, HD, 1), cosine, -sine)
    dv = dv_ref[...]
    dv = dv + pltpu.roll(dv, HD, 1)
    dall_ref[:, at_pair : at_pair + LANES] = jnp.where(lower, dk, dv).astype(bf16)

    dt = step_parts(proj_ref[:, at_step : at_step + LANES], bias_ref[...])
    linked = link_bias(seqc_ref[...], seqr_ref[...], False)
    decay = mm_exact(jnp.where(linked, 1.0, 0.0), -dt * rate_ref[...])
    decay_t = decay.T
    state = proj_ref[:, at_state : at_state + 256]
    sterms = conv_terms(state, masks)
    sconv = sum(t * convs_ref[k : k + 1, :] for k, t in enumerate(sterms))
    ssig = jax.nn.sigmoid(sconv)
    bcc = (sconv * ssig).astype(bf16)
    bm, cm = bcc[:, :128], bcc[:, 128:]
    gt_ref[...] = mm_nt(bm, cm)
    dgt_ref[...] = jnp.zeros_like(dgt_ref)
    for p in range(wp // LANES):
        cols = slice(p * LANES, (p + 1) * LANES)
        width = HD * min(2, heads - 2 * p)
        raw = proj_ref[:, wp + p * LANES : wp + (p + 1) * LANES]
        terms = conv_terms(raw, masks)
        conv = sum(t * convx_ref[k : k + 1, cols] for k, t in enumerate(terms))
        csig = jax.nn.sigmoid(conv)
        xc = conv * csig
        dt_cols = spread_heads(dt, 2 * p, width)
        xdt = (xc * dt_cols).astype(bf16)
        z = proj_ref[:, cols]
        zsig = jax.nn.sigmoid(z)
        dgated = dcat_ref[:, cols]
        scanned = scan_ref[:, cols]
        skip = skip_ref[:, cols]
        dy = dgated * (z * zsig)
        dall_ref[:, cols] = (dgated * (scanned + skip * xc) * (zsig * (1.0 + z * (1.0 - zsig)))).astype(bf16)
        gskip_ref[:, cols] = jnp.sum(dy * xc, axis=0, keepdims=True)
        dyb = dy.astype(bf16)
        blocks = []
        for a in range(rows // span):
            here = slice(a * span, (a + 1) * span)
            sides = []
            for side in range(width // HD):
                h = 2 * p + side
                dys = jnp.where(half_mask(rows - a * span, side), dyb[a * span :], jnp.zeros((), bf16))
                gap = decay_t[h : h + 1, a * span :] - decay[here, h : h + 1]
                falloff = jnp.exp(gap + neg_ref[here, a * span :])
                mixing = (gt_ref[here, a * span :] * falloff).astype(bf16)
                sides.append(mm(mixing, dyb[a * span :]))
                dgt_ref[here, a * span :] += mm_nt(xdt[here], dys) * falloff
            blocks.append(sides[0] if len(sides) == 1 else jnp.where(half_mask(span, 0), sides[0], sides[1]))
        dxdt = jnp.concatenate(blocks, axis=0)
        dsum_ref[:, cols] = dyb.astype(f32) * scanned - xdt.astype(f32) * dxdt
        ddir_ref[:, cols] = dxdt * xc
        dconv = (dxdt * dt_cols + skip * dy) * (csig * (1.0 + conv * (1.0 - csig)))
        gcx_ref[:, cols] = jnp.concatenate([jnp.sum(t * dconv, axis=0, keepdims=True) for t in terms], axis=0)
        dall_ref[:, wp + p * LANES : wp + (p + 1) * LANES] = conv_back(dconv, masks, convx_ref[:, cols]).astype(bf16)

    dgt = dgt_ref[...].astype(bf16)
    dbcc = jnp.concatenate([mm(dgt, cm), mm_tn(dgt, bm)], axis=1)
    dsconv = dbcc * (ssig * (1.0 + sconv * (1.0 - ssig)))
    gcs_ref[...] = jnp.concatenate([jnp.sum(t * dsconv, axis=0, keepdims=True) for t in sterms], axis=0)
    dall_ref[:, at_state : at_state + 256] = conv_back(dsconv, masks, convs_ref[...]).astype(bf16)

    head_of = lax.broadcasted_iota(jnp.int32, (wp, LANES), 0) // HD
    pick = jnp.where(head_of == lax.broadcasted_iota(jnp.int32, (wp, LANES), 1), 1.0, 0.0)
    ds = mm_exact(dsum_ref[...], pick)
    ddirect = mm_exact(ddir_ref[...], pick)
    dlog = mm_exact(jnp.where(linked_t, 1.0, 0.0), ds)
    rate = rate_ref[...]
    ddt = ddirect - rate * dlog
    dstep = ddt * jax.nn.sigmoid(proj_ref[:, at_step : at_step + LANES] + bias_ref[...])
    dstep = jnp.where(lane_ids(rows) < heads, dstep, 0.0)
    dall_ref[:, at_step : at_step + LANES] = dstep.astype(bf16)
    gstep_ref[...] = jnp.concatenate(
        [jnp.sum(dstep, axis=0, keepdims=True), -rate * jnp.sum(dt * dlog, axis=0, keepdims=True)], axis=0
    )
    dact = mm_nt(dall_ref[...], wcat_ref[...])
    dact_ref[...] = dact.astype(bf16)
    x = x_ref[...].astype(f32)
    r1 = lax.rsqrt(jnp.mean(x * x, axis=-1, keepdims=True) + norm_eps)
    gn1_ref[...] = jnp.sum(dact * x * r1, axis=0, keepdims=True)


def call(kernel, outs, scratch, args, flops):
    moved = sum(a.size * a.dtype.itemsize for a in args) + sum(s[0] * s[1] * jnp.dtype(t).itemsize for s, t in outs)
    return pl.pallas_call(
        kernel,
        out_shape=[jax.ShapeDtypeStruct(s, t) for s, t in outs],
        in_specs=[pl.BlockSpec(memory_space=pltpu.VMEM)] * len(args),
        out_specs=[pl.BlockSpec(memory_space=pltpu.VMEM)] * len(outs),
        scratch_shapes=[pltpu.VMEM(s, t) for s, t in scratch],
        compiler_params=pltpu.CompilerParams(vmem_limit_bytes=50 * 1024 * 1024),
        cost_estimate=pl.CostEstimate(flops=flops, bytes_accessed=moved, transcendentals=0),
    )(*args)


def swap(values):
    return lax.ppermute(values, "tensor", [(0, 1), (1, 0)])


def gather_rows(values, me, count):
    if count != 2:
        return lax.all_gather(values, "tensor", axis=0, tiled=True)
    other = swap(values)
    first = jnp.where(me == 0, values, other)
    return jnp.concatenate([first, jnp.where(me == 0, other, values)], axis=0)


def both_parts(part, count):
    if count != 2:
        return (lax.psum(part, "tensor"), jnp.zeros_like(part))
    return (part, swap(part))


def scatter_rows(part, me, count):
    if count != 2:
        return lax.psum_scatter(part, "tensor", scatter_dimension=0, tiled=True).astype(f32)
    halves = part.reshape(2, part.shape[0] // 2, part.shape[1])
    arrived = swap(lax.dynamic_index_in_dim(halves, 1 - me, 0, keepdims=False))
    return lax.dynamic_index_in_dim(halves, me, 0, keepdims=False).astype(f32) + arrived.astype(f32)


def partners(count, bit):
    return [(i, i ^ bit) for i in range(count)]


def weight_halves(left_t, right, index, count):
    features = left_t.shape[0]
    blocks = left_t.reshape(count // 2, 2, features // count, left_t.shape[1])
    bit = index % 2

    def part(which):
        chosen = lax.dynamic_index_in_dim(blocks, which, 1, keepdims=False).reshape(features // 2, -1)
        return mm(chosen, right).astype(bf16)

    return part(1 - bit), part(bit)


def halving(sent, kept, index, count):
    arrived = lax.ppermute(sent, "dp", partners(count, 1))
    held = kept.astype(f32) + arrived.astype(f32)
    left, bit = count // 2, 2
    while left > 1:
        blocks = held.astype(bf16).reshape(left // 2, 2, held.shape[0] // left, held.shape[1])
        which = (index // bit) % 2
        away = lax.dynamic_index_in_dim(blocks, 1 - which, 1, keepdims=False).reshape(held.shape[0] // 2, -1)
        mine = lax.dynamic_index_in_dim(blocks, which, 1, keepdims=False).reshape(held.shape[0] // 2, -1)
        arrived = lax.ppermute(away, "dp", partners(count, bit))
        held = mine.astype(f32) + arrived.astype(f32)
        left, bit = left // 2, bit * 2
    return held


def doubling(values, count):
    bit = 1
    while bit < count:
        values = values + lax.ppermute(values, "dp", partners(count, bit))
        bit *= 2
    return values


def segments(lengths, row_count):
    seq_ends = jnp.cumsum(lengths)
    places = jnp.arange(row_count, dtype=jnp.int32)
    passed = places[:, None] >= seq_ends[None, :]
    seq_ids = jnp.sum(passed.astype(jnp.int32), axis=1)
    starts = jnp.max(jnp.where(passed, seq_ends[None, :], 0), axis=1)
    is_live = (places < seq_ends[-1]).astype(f32)
    return (seq_ids, places - starts, is_live)


def body(
    dp_count, tensor_count, tokens, cotangent, seq_lengths, norm1_gain, norm2_gain, mixer_in, state_in, step_in,
    conv_inner, conv_state, step_bias, decay_log, skip_gain, mixer_out, query_in, key_value, attend_out, gate_up,
    down_out,
):
    share, model = tokens.shape
    rows = share * tensor_count
    me = lax.axis_index("tensor")
    index = lax.axis_index("dp")
    inner = mixer_in.shape[2]
    heads = step_in.shape[1]
    query_width = query_in.shape[1]
    qheads = query_width // HD
    wp, qwp = padded(inner), padded(query_width)
    span = min(LANES, rows)
    dims = (heads, qheads, wp, qwp, span)
    columns = 2 * wp + 384 + qwp + LANES

    x_rows = gather_rows(tokens, me, tensor_count)
    seq_ids, positions, is_live = segments(seq_lengths[0], rows)
    live_share = lax.dynamic_slice_in_dim(is_live, me * share, share, 0)[:, None]
    grad_out = cotangent.astype(f32) * live_share
    dout_rows = gather_rows(grad_out.astype(bf16), me, tensor_count)

    seq_col = seq_ids.astype(f32)[:, None]
    seq_row = seq_ids.astype(f32)[None, :]
    shifts = jnp.minimum(jnp.arange(LANES, dtype=jnp.int32), 4)[None, :]
    masks = (positions[:, None] >= shifts).astype(f32)
    lane = jnp.arange(LANES)
    frequency = rope_base ** (-2.0 * jnp.arange(HD // 2, dtype=f32) / HD)
    angles = positions.astype(f32)[:, None] * frequency[None, :]
    cosine = jnp.tile(jnp.cos(angles), (1, 4))
    sine = jnp.tile(jnp.sin(angles), (1, 4)) * jnp.where(lane % HD < HD // 2, -1.0, 1.0)[None, :]

    key_index = me * qheads // (QH // KVH)
    pair_local = lax.dynamic_slice_in_dim(key_value, key_index * HD, HD, 2).reshape(model, 2 * HD)
    wcat = jnp.concatenate(
        [
            pad_to(mixer_in[:, 0], wp), pad_to(mixer_in[:, 1], wp), state_in, pad_to(step_in, LANES),
            pad_to(query_in, qwp), pair_local,
        ],
        axis=1,
    )
    wout = jnp.concatenate([pad_to(mixer_out, wp), pad_to(attend_out, qwp)], axis=1)
    wgu = gate_up.reshape(model, -1)
    taps = pad_to(conv_inner, wp)
    bias = pad_to(step_bias[None], LANES)
    rate = pad_to(jnp.exp(decay_log)[None], LANES)
    skip = pad_to(jnp.repeat(skip_gain, HD)[None], wp)
    gain1, gain2 = norm1_gain[None], norm2_gain[None]

    act, proj, scanned, cat, part = call(
        functools.partial(front_kernel, dims),
        [((rows, model), bf16), ((rows, columns), f32), ((rows, wp), f32), ((rows, wp + qwp), bf16), ((rows, model), bf16)],
        [((rows, rows), f32), ((rows, rows), f32), ((rows, LANES), bf16)],
        (x_rows, gain1, wcat, wout, seq_col, seq_row, masks, cosine, sine, taps, conv_state, bias, rate, skip),
        8 * rows * model * columns,
    )
    dhidden = mm(dout_rows, down_out)
    own, other = both_parts(part, tensor_count)
    ff2 = wgu.shape[1]
    h1, n2, hidden, dgu, ffn_part, dn2_part = call(
        middle_kernel,
        [
            ((rows, model), f32), ((rows, model), bf16), ((rows, ff2 // 2), bf16), ((rows, ff2), bf16),
            ((rows, model), bf16), ((rows, model), bf16),
        ],
        [],
        (x_rows, own, other, gain2, wgu, down_out, dhidden),
        6 * rows * model * ff2,
    )
    dn2_own, dn2_other = both_parts(dn2_part, tensor_count)
    ffn_share = scatter_rows(ffn_part, me, tensor_count)
    h1_share = lax.dynamic_slice_in_dim(h1, me * share, share, 0)
    block_out = ((h1_share + ffn_share) * live_share).astype(bf16)

    up_sent, up_kept = weight_halves(n2.T, dgu, index, dp_count)
    down_sent, down_kept = weight_halves(dout_rows.T, hidden, index, dp_count)
    ffn_total = halving(
        jnp.concatenate([up_sent, down_sent], axis=1), jnp.concatenate([up_kept, down_kept], axis=1), index, dp_count
    )

    dh1, dmix, dall, dact, gn1, gn2, gcx, gcs, gstep, gskip = call(
        functools.partial(back_kernel, dims),
        [
            ((rows, model), f32), ((rows, model), bf16), ((rows, columns), bf16), ((rows, model), bf16),
            ((1, model), f32), ((1, model), f32), ((4, wp), f32), ((4, 256), f32), ((2, LANES), f32), ((1, wp), f32),
        ],
        [
            ((rows, rows), f32), ((rows, rows), f32), ((rows, rows), f32), ((rows, wp + qwp), f32),
            ((rows, wp), f32), ((rows, wp), f32), ((rows, LANES), f32), ((rows, LANES), f32),
        ],
        (
            dn2_own, dn2_other, h1, dout_rows, gain2, x_rows, wcat, wout, seq_col, seq_row, masks, cosine, sine, taps,
            conv_state, bias, rate, skip, proj, scanned,
        ),
        12 * rows * model * columns,
    )
    out_sent, out_kept = weight_halves(dmix.T, cat, index, dp_count)
    out_total = halving(out_sent, out_kept, index, dp_count)
    in_sent, in_kept = weight_halves(act.T, dall, index, dp_count)
    in_total = halving(in_sent, in_kept, index, dp_count)

    dact_share = scatter_rows(dact, me, tensor_count)
    x_share = tokens.astype(f32)
    r1 = lax.rsqrt(jnp.mean(x_share * x_share, axis=-1, keepdims=True) + norm_eps)
    u = dact_share * gain1
    dh1_share = lax.dynamic_slice_in_dim(dh1, me * share, share, 0)
    token_grad = dh1_share + r1 * u - x_share * (r1 * r1 * r1 * jnp.mean(u * x_share, axis=-1, keepdims=True))

    shared = jnp.concatenate([gn1[0], gn2[0] * (1.0 / tensor_count), gcs.reshape(-1)]).reshape(-1, LANES)
    local = jnp.concatenate([gcx.reshape(-1), gskip.reshape(-1), gstep.reshape(-1)]).reshape(-1, LANES)
    minor = doubling(jnp.concatenate([shared, local], axis=0), dp_count)
    shared_rows = shared.shape[0]
    shared = lax.psum(minor[:shared_rows], "tensor") if tensor_count != 2 else minor[:shared_rows] + swap(minor[:shared_rows])
    shared = shared.reshape(-1)
    local = minor[shared_rows:].reshape(-1)
    g_norm1, g_norm2, g_conv_state = shared[:model], shared[model : 2 * model], shared[2 * model :].reshape(4, 256)
    g_conv_inner = local[: 4 * wp].reshape(4, wp)[:, :inner]
    g_skip = jnp.sum(local[4 * wp : 5 * wp].reshape(-1, HD), axis=1)[:heads]
    g_bias = local[5 * wp : 5 * wp + heads]
    g_decay = local[5 * wp + LANES : 5 * wp + LANES + heads]

    block = in_total.shape[0]
    both = jnp.concatenate([in_total[:, 2 * wp : 2 * wp + 256], in_total[:, columns - LANES :]], axis=1).astype(bf16)
    placed = lambda pair: lax.dynamic_update_slice_in_dim(
        jnp.zeros((block,) + key_value.shape[1:], f32), pair.astype(f32).reshape(block, 2, HD), key_index * HD, 2
    )
    if tensor_count == 2:
        arrived = swap(both)
        g_state = both[:, :256].astype(f32) + arrived[:, :256].astype(f32)
        mine = both[:, 256:].reshape(block, 2, HD)
        theirs = arrived[:, 256:].reshape(block, 2, HD)
        g_pair = jnp.concatenate(
            [jnp.where(me == 0, mine, theirs), jnp.where(me == 0, theirs, mine)], axis=2
        ).astype(f32)
    else:
        g_state = lax.psum(both[:, :256], "tensor").astype(f32)
        g_pair = lax.psum(placed(both[:, 256:]).astype(bf16), "tensor").astype(f32)

    g_mixer_in = jnp.stack([in_total[:, :inner], in_total[:, wp : wp + inner]], axis=1)
    at_step = 2 * wp + 256
    at_query = at_step + LANES
    return (
        block_out,
        token_grad.astype(bf16),
        g_norm1,
        g_norm2,
        g_mixer_in,
        g_state,
        in_total[:, at_step : at_step + heads],
        g_conv_inner,
        g_conv_state,
        g_bias,
        g_decay,
        g_skip,
        out_total[:, :inner],
        in_total[:, at_query : at_query + query_width],
        g_pair,
        out_total[:, wp : wp + query_width],
        ffn_total[:, :ff2].reshape(block, 2, ff2 // 2),
        ffn_total[:, ff2:],
    )


def solution(mesh):
    return jax.shard_map(
        functools.partial(body, mesh.shape["dp"], mesh.shape["tensor"]),
        mesh=mesh,
        in_specs=(
            P(("dp", "tensor"), None),
            P(("dp", "tensor"), None),
            P("dp", None),
            P(),
            P(),
            P(None, None, "tensor"),
            P(),
            P(None, "tensor"),
            P(None, "tensor"),
            P(),
            P("tensor"),
            P("tensor"),
            P("tensor"),
            P(None, "tensor"),
            P(None, "tensor"),
            P(),
            P(None, "tensor"),
            P(None, None, "tensor"),
            P(None, "tensor"),
        ),
        out_specs=(
            P(("dp", "tensor"), None),
            P(("dp", "tensor"), None),
            P(),
            P(),
            P("dp", None, "tensor"),
            P("dp", None),
            P("dp", "tensor"),
            P(None, "tensor"),
            P(),
            P("tensor"),
            P("tensor"),
            P("tensor"),
            P("dp", "tensor"),
            P("dp", "tensor"),
            P("dp", None, None),
            P("dp", "tensor"),
            P("dp", None, "tensor"),
            P("dp", "tensor"),
        ),
        check_vma=False,
    )
```

time: 1230 us -> 282 us (0.23)
  waiting for transfers between devices: 680 us -> 120 us
  matrix products: 137 us -> 16.9 us
  local copies, waits for them, and re-layouts: 163 us -> 46.4 us
  blocking collectives: 116 us -> 0 us
  other arithmetic: 105 us -> 24.8 us
  Pallas kernels: 0 us -> 44.2 us
  starting transfers between devices: 0.58 us -> 24.9 us
  between operations: 16.2 us -> 2.12 us
    reduce_scatter x11 -> x0, waiting for transfers between devices: 431 us -> none  [the longest x1 74.2 us: send_ffn(): lax.psum_scatter(grad_gate_up.astype(jnp.bfloat16), 'dp', scatter_dimensi...]
    unnamed x16 -> x0, waiting for transfers between devices: 228 us -> none
    dot_general x75 -> x9, matrix products: 137 us -> 16.9 us  [mm(): return jnp.dot(left, right, preferred_element_type=f32)]
    ppermute x0 -> x24, waiting for transfers between devices: none -> 120 us  [the longest x9 90.4 us: halving(): arrived = lax.ppermute(away, 'dp', partners(count, bit))]
    psum x1 -> x0, blocking collectives: 60.8 us -> none  [body(): lax.psum((grad_norm1, grad_norm2, grads_mixer[4], grad_conv_state, grads_...]
    all_gather x4 -> x0, blocking collectives: 55.2 us -> none  [the longest x1 19.5 us: body(): grad_out_rows = lax.all_gather(grad_out_b, 'tensor', axis=0, tiled=True)]
    pallas_call x0 -> x3, Pallas kernels: none -> 44.2 us  [call(): pl.pallas_call(kernel, out_shape=[jax.ShapeDtypeStruct(s, t) for s, t in...]
    dynamic_update_slice x1 -> x0, local copies, waits for them, and re-layouts: 31.6 us -> none  [body(): lax.dynamic_update_slice_in_dim(jnp.zeros(key_value.shape, jnp.float32),...]
  transfers between devices with their start and end apart: 14 -> 24, of which waited for: 14 -> 10; matrix products, arithmetic and copies ran while one was open for 7% -> 25% of each run, Pallas kernels for 0% -> 8%
where the time goes in v1:
time: 282 us; the launch traced here: 280 us
  waiting for transfers between devices  120 us (43%)
  local copies, waits for them, and re-layouts  46.4 us (16%)
  Pallas kernels  44.2 us (16%)
  starting transfers between devices  24.9 us (9%)
  other arithmetic  24.8 us (9%)
  matrix products  16.9 us (6%)
    ppermute x9, waiting for transfers between devices, halving(): arrived = lax.ppermute(away, 'dp', partners(count, bit))  90.4 us
    pallas_call x3, Pallas kernels, call(): pl.pallas_call(kernel, out_shape=[jax.ShapeDtypeStruct(s, t) for s, t in...  44.2 us
    ppermute x8, waiting for transfers between devices, swap(): return lax.ppermute(values, 'tensor', [(0, 1), (1, 0)])  29.9 us
    unnamed x113, local copies, waits for them, and re-layouts  20.2 us
    dot_general x9, matrix products, mm(): return jnp.dot(left, right, preferred_element_type=f32)  16.9 us
    ppermute x8, starting transfers between devices, swap(): return lax.ppermute(values, 'tensor', [(0, 1), (1, 0)])  10.4 us
    slice x1, local copies, waits for them, and re-layouts, body(): mixer_in[:, 1]  7.91 us
    ppermute x9, starting transfers between devices, halving(): arrived = lax.ppermute(away, 'dp', partners(count, bit))  7.82 us
  transfers between devices with their start and end apart: 24, of which 10 were waited for; matrix products, arithmetic and copies ran while one was open for 25% of the time, Pallas kernels for 8%

profile of v1, /device:TPU:0, one launch (start us, length us, event | category | flops | bytes accessed | tf_op | source)
XLA Modules:
  0.0 279.6 jit_solution(18180768068771043351)
XLA Ops:
  3.4 1.9 multiply_convert_fusion
  5.3 3.0 %collective-permute-start.2 = (bf16[192,1024]{1,0:T(8,128)(2,1)}, bf16[192,1024]{1,0:T(8,128)(2,1)}, u32[]{:S(2)}, u32[]{:S(2)}) collective-permute-start(bf16[192,1024]{1,0:T(8,128)(2,1)} %multiply_convert_fusion), channel_id=1, source_target_pairs={{0,1},{1,0},{2,3},{3,2},{4,5},{5,4},{6,7},{7,6},{8,9},{9,8},{10,11... | collective-permute-start | bytes 1179656 | tf_op jit(solution)/shard_map/ppermute | solution.py:349
  9.6 7.9 %fusion.23 = (bf16[1024,1,768]{2,1,0:T(2,128)(2,1)S(1)}, bf16[1024,1,768]{2,1,0:T(2,128)(2,1)S(1)}) fusion(bf16[1024,2,768]{2,1,0:T(2,128)(2,1)} %param.24), kind=kLoop, calls=%fused_computation.121 | loop fusion | bytes 6291456 | tf_op jit(solution)/shard_map/slice | solution.py:461
  20.0 2.7 constant_dynamic-update-slice_fusion.4
  29.6 2.3 broadcast_select_fusion.1
  32.0 14.0 %shard_map.322 = (bf16[384,1024]{1,0:T(8,128)(2,1)S(1)}, f32[384,2304]{1,0:T(8,128)}, f32[384,768]{1,0:T(8,128)}, bf16[384,1024]{1,0:T(8,128)(2,1)S(1)}, bf16[384,1024]{1,0:T(8,128)(2,1)}) custom-call(bf16[384,1024]{1,0:T(8,128)(2,1)S(1)} %pad_maximum_fusion.1.x_ref, f32[1,1024]{1,0:T(1,128)S(1)} %bitcast.152, ...), custom_call_target="tpu_custom_call" | custom-call | flops 7247757312 | bytes 15297536 | tf_op jit(solution)/shard_map/pallas_call | solution.py:337
  46.0 2.0 collective-permute-start.1
  48.0 5.6 %copy.101 = bf16[128,8,2,1024]{3,1,2,0:T(8,128)(2,1)} copy(bf16[128,8,2,1024]{3,2,1,0:T(2,128)(2,1)} %bitcast.163) | data formatting | bytes 8388608
  53.6 2.2 fusion.20
  57.4 2.4 constant_dynamic-slice_fusion.6
  60.8 2.2 fusion.21.dhid_ref
  62.9 2.4 collective-permute-done.1.other_ref
  65.3 8.5 %shard_map.323 = (f32[384,1024]{1,0:T(8,128)}, bf16[384,1024]{1,0:T(8,128)(2,1)S(1)}, bf16[384,1024]{1,0:T(8,128)(2,1)S(1)}, bf16[384,2048]{1,0:T(8,128)(2,1)}, ...) custom-call(bf16[384,1024]{1,0:T(8,128)(2,1)S(1)} %pad_maximum_fusion.1.x_ref, ...), custom_call_target="tpu_custom_call" | custom-call | flops 4831838208 | bytes 16519168 | tf_op jit(solution)/shard_map/pallas_call | solution.py:337
  76.1 2.7 convolution_convert_fusion.2
  79.6 1.9 pad_maximum_fusion
  85.4 2.6 convolution_convert_fusion.3
  88.0 21.8 %collective-permute-done.3 = bf16[192,1024]{1,0:T(8,128)(2,1)S(1)} collective-permute-done((bf16[192,1024]{1,0:T(8,128)(2,1)S(1)}, bf16[192,1024]{1,0:T(8,128)(2,1)S(1)}, u32[]{:S(2)}, u32[]{:S(2)}) %collective-permute-start.3) | collective-permute-done | bytes 393248 | tf_op jit(solution)/shard_map/ppermute | solution.py:349
  110.8 21.8 %shard_map.324 = (f32[384,1024]{1,0:T(8,128)}, bf16[384,1024]{1,0:T(8,128)(2,1)S(1)}, bf16[384,2304]{1,0:T(8,128)(2,1)}, bf16[384,1024]{1,0:T(8,128)(2,1)S(1)}, ...) custom-call(bf16[384,1024]{1,0:T(8,128)(2,1)S(1)} %copy-done.11, ...), custom_call_target="tpu_custom_call" | custom-call | flops 10871635968 | bytes 21814272 | tf_op jit(solution)/shard_map/pallas_call | solution.py:337
  137.0 2.8 convolution_convert_fusion.1
  141.4 2.8 %convolution_convert_fusion = bf16[512,2304]{1,0:T(8,128)(2,1)} fusion(bf16[512,384]{1,0:T(8,128)(2,1)S(1)} %bitcast.188, bf16[384,2304]{1,0:T(8,128)(2,1)S(1)} %copy-done.50), kind=kOutput, calls=%fused_computation.2 | convolution fusion | flops 907149312 | bytes 4521984 | tf_op jit(solution)/shard_map/dot_general | solution.py:32
  144.3 2.7 collective-permute-start.9
  153.9 5.6 %collective-permute-done.10 = f32[24,128]{1,0:T(8,128)} collective-permute-done((f32[24,128]{1,0:T(8,128)S(1)}, f32[24,128]{1,0:T(8,128)}, u32[]{:S(2)}, u32[]{:S(2)}) %collective-permute-start.10) | collective-permute-done | bytes 12320 | tf_op jit(solution)/shard_map/ppermute | solution.py:349
  162.1 3.0 %collective-permute-done.17 = bf16[256,1024]{1,0:T(8,128)(2,1)S(1)} collective-permute-done((bf16[256,1024]{1,0:T(8,128)(2,1)S(1)}, bf16[256,1024]{1,0:T(8,128)(2,1)S(1)}, u32[]{:S(2)}, u32[]{:S(2)}) %collective-permute-start.17) | collective-permute-done | bytes 524320 | tf_op jit(solution)/shard_map/ppermute | solution.py:399
  167.0 5.3 %collective-permute-done.18 = bf16[128,1024]{1,0:T(8,128)(2,1)S(1)} collective-permute-done((bf16[128,1024]{1,0:T(8,128)(2,1)S(1)}, bf16[128,1024]{1,0:T(8,128)(2,1)S(1)}, u32[]{:S(2)}, u32[]{:S(2)}) %collective-permute-start.18) | collective-permute-done | bytes 262176 | tf_op jit(solution)/shard_map/ppermute | solution.py:399
  174.2 2.2 add_convert_fusion.1
  178.3 3.0 %add_convert_fusion = bf16[512,3072]{1,0:T(8,128)(2,1)S(1)} fusion(bf16[512,3072]{1,0:T(8,128)(2,1)} %collective-permute-done.20, bf16[512,1024]{1,0:T(8,128)(2,1)S(1)} %copy-done.21, bf16[512,2048]{1,0:T(8,128)(2,1)S(1)} %copy-done.25), kind=kLoop, calls=%fused_computation | loop fusion | flops 11010048 | bytes 9437184 | tf_op jit(solution)/shard_map/convert_element_type | solution.py:395
  182.8 2.0 fusion.10
  186.2 19.4 %collective-permute-done.12 = bf16[256,2304]{1,0:T(8,128)(2,1)S(1)} collective-permute-done((bf16[256,2304]{1,0:T(8,128)(2,1)S(1)}, bf16[256,2304]{1,0:T(8,128)(2,1)S(1)}, u32[]{:S(2)}, u32[]{:S(2)}) %collective-permute-start.12) | collective-permute-done | bytes 1179680 | tf_op jit(solution)/shard_map/ppermute | solution.py:399
  206.4 28.9 %collective-permute-done.21 = bf16[256,3072]{1,0:T(8,128)(2,1)S(1)} collective-permute-done((bf16[256,3072]{1,0:T(8,128)(2,1)S(1)}, bf16[256,3072]{1,0:T(8,128)(2,1)S(1)}, u32[]{:S(2)}, u32[]{:S(2)}) %collective-permute-start.21) | collective-permute-done | bytes 1572896 | tf_op jit(solution)/shard_map/ppermute | solution.py:399
  238.6 9.7 %collective-permute-done.14 = bf16[64,2304]{1,0:T(8,128)(2,1)S(1)} collective-permute-done((bf16[64,2304]{1,0:T(8,128)(2,1)S(1)}, bf16[64,2304]{1,0:T(8,128)(2,1)S(1)}, u32[]{:S(2)}, u32[]{:S(2)}) %collective-permute-start.14) | collective-permute-done | bytes 294944 | tf_op jit(solution)/shard_map/ppermute | solution.py:399
  251.1 8.9 %collective-permute-done.22 = bf16[128,3072]{1,0:T(8,128)(2,1)S(1)} collective-permute-done((bf16[128,3072]{1,0:T(8,128)(2,1)S(1)}, bf16[128,3072]{1,0:T(8,128)(2,1)S(1)}, u32[]{:S(2)}, u32[]{:S(2)}) %collective-permute-start.22) | collective-permute-done | bytes 786464 | tf_op jit(solution)/shard_map/ppermute | solution.py:399
  261.9 15.1 %collective-permute-done.23 = bf16[64,3072]{1,0:T(8,128)(2,1)S(1)} collective-permute-done((bf16[64,3072]{1,0:T(8,128)(2,1)S(1)}, bf16[64,3072]{1,0:T(8,128)(2,1)S(1)}, u32[]{:S(2)}, u32[]{:S(2)}) %collective-permute-start.23) | collective-permute-done | bytes 393248 | tf_op jit(solution)/shard_map/ppermute | solution.py:399
  (246 shorter events, 58.2 us)
Async XLA Ops:
  5.3 24.2 %collective-permute-start.2 = (bf16[192,1024]{1,0:T(8,128)(2,1)}, bf16[192,1024]{1,0:T(8,128)(2,1)}, u32[]{:S(2)}, u32[]{:S(2)}) collective-permute-start(bf16[192,1024]{1,0:T(8,128)(2,1)} %multiply_convert_fusion), channel_id=1, source_target_pairs={{0,1},{1,0},{2,3},{3,2},{4,5},{5,4},{6,7},{7,6},{8,9},{9,8},{10,11... | collective-permute-start | bytes 1179656 | tf_op jit(solution)/shard_map/ppermute | solution.py:349
  8.3 21.3 %collective-permute-start = (bf16[192,1024]{1,0:T(8,128)(2,1)}, bf16[192,1024]{1,0:T(8,128)(2,1)}, u32[]{:S(2)}, u32[]{:S(2)}) collective-permute-start(bf16[192,1024]{1,0:T(8,128)(2,1)} %param.19), channel_id=1, source_target_pairs={{0,1},{1,0},{2,3},{3,2},{4,5},{5,4},{6,7},{7,6},{8,9},{9,8},{10,11... | collective-permute-start | bytes 1179656 | tf_op jit(solution)/shard_map/ppermute | solution.py:349
  31.9 33.4 %copy-start.2 = (bf16[384,1024]{1,0:T(8,128)(2,1)}, bf16[384,1024]{1,0:T(8,128)(2,1)S(1)}, u32[]{:S(2)}) copy-start(bf16[384,1024]{1,0:T(8,128)(2,1)S(1)} %pad_maximum_fusion.1.x_ref) | copy-start | bytes 2359300
  46.0 19.3 %collective-permute-start.1 = (bf16[384,1024]{1,0:T(8,128)(2,1)}, bf16[384,1024]{1,0:T(8,128)(2,1)}, u32[]{:S(2)}, u32[]{:S(2)}) collective-permute-start(bf16[384,1024]{1,0:T(8,128)(2,1)} %get-tuple-element.39.own_ref), channel_id=1, source_target_pairs={{0,1},{1,0},{2,3},{3,2},{4,5},{5,4},{6,7},{7,6},{8,9},{9,8},{10,11... | collective-permute-start | bytes 2359304 | tf_op jit(solution)/shard_map/ppermute | solution.py:349
  81.4 96.3 %collective-permute-start.20 = (bf16[512,3072]{1,0:T(8,128)(2,1)}, bf16[512,3072]{1,0:T(8,128)(2,1)}, u32[]{:S(2)}, u32[]{:S(2)}) collective-permute-start(bf16[512,3072]{1,0:T(8,128)(2,1)} %pad_maximum_fusion), channel_id=1, source_target_pairs={{0,2},{2,0},{4,6},{6,4},{8,10},{10,8},{12,14},{14,12},{16,18},{18,... | collective-permute-start | bytes 9437192 | tf_op jit(solution)/shard_map/ppermute | solution.py:391
  81.4 29.3 %collective-permute-start.4 = (bf16[384,1024]{1,0:T(8,128)(2,1)S(1)}, bf16[384,1024]{1,0:T(8,128)(2,1)S(1)}, u32[]{:S(2)}, u32[]{:S(2)}) collective-permute-start(bf16[384,1024]{1,0:T(8,128)(2,1)S(1)} %copy-done.11), channel_id=1, source_target_pairs={{0,1},{1,0},{2,3},{3,2},{4,5},{5,4},{6,7},{7,6},{8,9},{9,8},{10,11... | collective-permute-start | bytes 2359304 | tf_op jit(solution)/shard_map/ppermute | solution.py:349
  83.3 26.6 %collective-permute-start.3 = (bf16[192,1024]{1,0:T(8,128)(2,1)S(1)}, bf16[192,1024]{1,0:T(8,128)(2,1)S(1)}, u32[]{:S(2)}, u32[]{:S(2)}) collective-permute-start(bf16[192,1024]{1,0:T(8,128)(2,1)S(1)} %dynamic-slice_bitcast_fusion.2), channel_id=1, source_target_pairs={{0,1},{1,0},{2,3},{3,2},{4,5},{5,4},{6,7},{7,6},{8,9},{9,8},{10,11... | collective-permute-start | bytes 1179656 | tf_op jit(solution)/shard_map/ppermute | solution.py:349
  85.3 24.5 %copy-start.44 = (f32[192]{0:T(256)S(1)}, f32[192]{0:T(256)}, u32[]{:S(2)}) copy-start(f32[192]{0:T(256)} %copy-done.42) | copy-start | bytes 2308
  85.3 25.4 %copy-start.6 = (f32[384,128]{1,0:T(8,128)S(1)}, f32[384,128]{1,0:T(8,128)}, u32[]{:S(2)}) copy-start(f32[384,128]{1,0:T(8,128)} %copy-done.5) | copy-start | bytes 589828
  85.3 25.4 %copy-start.8 = (f32[384,128]{1,0:T(8,128)S(1)}, f32[384,128]{1,0:T(8,128)}, u32[]{:S(2)}) copy-start(f32[384,128]{1,0:T(8,128)} %copy-done.7) | copy-start | bytes 589828
  85.3 25.4 %copy-start.13 = (f32[4,768]{1,0:T(4,128)S(1)}, f32[4,768]{1,0:T(4,128)}, u32[]{:S(2)}) copy-start(f32[4,768]{1,0:T(4,128)} %convx_ref.3) | copy-start | bytes 36868
  85.3 25.4 %copy-start.16 = (f32[1024]{0:T(1024)S(1)}, f32[1024]{0:T(1024)}, u32[]{:S(2)}) copy-start(f32[1024]{0:T(1024)} %param.23) | copy-start | bytes 12292
  85.4 25.4 %copy-start.18 = (f32[1,128]{1,0:T(1,128)S(1)}, f32[1,128]{1,0:T(1,128)}, u32[]{:S(2)}) copy-start(f32[1,128]{1,0:T(1,128)} %copy-done.17) | copy-start | bytes 1540
  85.4 25.4 %copy-start.20 = (f32[1,128]{1,0:T(1,128)S(1)}, f32[1,128]{1,0:T(1,128)}, u32[]{:S(2)}) copy-start(f32[1,128]{1,0:T(1,128)} %copy-done.19) | copy-start | bytes 1540
  133.9 1.4 collective-permute-start.6
  134.6 16.1 %collective-permute-start.16 = (bf16[512,1024]{1,0:T(8,128)(2,1)S(1)}, bf16[512,1024]{1,0:T(8,128)(2,1)S(1)}, u32[]{:S(2)}, u32[]{:S(2)}) collective-permute-start(bf16[512,1024]{1,0:T(8,128)(2,1)S(1)} %convolution_convert_fusion.6), channel_id=1, source_target_pairs={{0,2},{2,0},{4,6},{6,4},{8,10},{10,8},{12,14},{14,12},{16,18},{18,... | collective-permute-start | bytes 3145736 | tf_op jit(solution)/shard_map/ppermute | solution.py:391
  135.2 4.6 %collective-permute-start.7 = (f32[56,128]{1,0:T(8,128)S(1)}, f32[56,128]{1,0:T(8,128)S(1)}, u32[]{:S(2)}, u32[]{:S(2)}) collective-permute-start(f32[56,128]{1,0:T(8,128)S(1)} %fusion.19), channel_id=1, source_target_pairs={{0,4},{2,6},{4,0},{6,2},{8,12},{10,14},{12,8},{14,10},{16,20},{18,... | collective-permute-start | bytes 86024 | tf_op jit(solution)/shard_map/ppermute | solution.py:408
  139.8 4.5 %collective-permute-start.8 = (f32[56,128]{1,0:T(8,128)S(1)}, f32[56,128]{1,0:T(8,128)S(1)}, u32[]{:S(2)}, u32[]{:S(2)}) collective-permute-start(f32[56,128]{1,0:T(8,128)S(1)} %add.208), channel_id=1, source_target_pairs={{0,8},{2,10},{4,12},{6,14},{8,0},{10,2},{12,4},{14,6},{16,24},{18,... | collective-permute-start | bytes 86024 | tf_op jit(solution)/shard_map/ppermute | solution.py:408
  144.2 30.0 %collective-permute-start.11 = (bf16[512,2304]{1,0:T(8,128)(2,1)}, bf16[512,2304]{1,0:T(8,128)(2,1)}, u32[]{:S(2)}, u32[]{:S(2)}) collective-permute-start(bf16[512,2304]{1,0:T(8,128)(2,1)} %convolution_convert_fusion), channel_id=1, source_target_pairs={{0,2},{2,0},{4,6},{6,4},{8,10},{10,8},{12,14},{14,12},{16,18},{18,... | collective-permute-start | bytes 7077896 | tf_op jit(solution)/shard_map/ppermute | solution.py:391
  144.3 5.0 %collective-permute-start.9 = (f32[56,128]{1,0:T(8,128)S(1)}, f32[56,128]{1,0:T(8,128)S(1)}, u32[]{:S(2)}, u32[]{:S(2)}) collective-permute-start(f32[56,128]{1,0:T(8,128)S(1)} %add.209), channel_id=1, source_target_pairs={{0,16},{2,18},{4,20},{6,22},{8,24},{10,26},{12,28},{14,30},{16,0},... | collective-permute-start | bytes 86024 | tf_op jit(solution)/shard_map/ppermute | solution.py:408
  147.7 17.7 %collective-permute-start.5 = (bf16[192,1024]{1,0:T(8,128)(2,1)}, bf16[192,1024]{1,0:T(8,128)(2,1)}, u32[]{:S(2)}, u32[]{:S(2)}) collective-permute-start(bf16[192,1024]{1,0:T(8,128)(2,1)} %dynamic-slice_bitcast_fusion.1), channel_id=1, source_target_pairs={{0,1},{1,0},{2,3},{3,2},{4,5},{5,4},{6,7},{7,6},{8,9},{9,8},{10,11... | collective-permute-start | bytes 1179656 | tf_op jit(solution)/shard_map/ppermute | solution.py:349
  149.3 10.2 %collective-permute-start.10 = (f32[24,128]{1,0:T(8,128)S(1)}, f32[24,128]{1,0:T(8,128)}, u32[]{:S(2)}, u32[]{:S(2)}) collective-permute-start(f32[24,128]{1,0:T(8,128)S(1)} %slice.115), channel_id=1, source_target_pairs={{0,1},{1,0},{2,3},{3,2},{4,5},{5,4},{6,7},{7,6},{8,9},{9,8},{10,11... | collective-permute-start | bytes 36872 | tf_op jit(solution)/shard_map/ppermute | solution.py:349
  151.6 13.5 %collective-permute-start.17 = (bf16[256,1024]{1,0:T(8,128)(2,1)S(1)}, bf16[256,1024]{1,0:T(8,128)(2,1)S(1)}, u32[]{:S(2)}, u32[]{:S(2)}) collective-permute-start(bf16[256,1024]{1,0:T(8,128)(2,1)S(1)} %bitcast.187), channel_id=1, source_target_pairs={{0,4},{2,6},{4,0},{6,2},{8,12},{10,14},{12,8},{14,10},{16,20},{18,... | collective-permute-start | bytes 1572872 | tf_op jit(solution)/shard_map/ppermute | solution.py:399
  165.3 6.9 %collective-permute-start.18 = (bf16[128,1024]{1,0:T(8,128)(2,1)S(1)}, bf16[128,1024]{1,0:T(8,128)(2,1)S(1)}, u32[]{:S(2)}, u32[]{:S(2)}) collective-permute-start(bf16[128,1024]{1,0:T(8,128)(2,1)S(1)} %bitcast.192), channel_id=1, source_target_pairs={{0,8},{2,10},{4,12},{6,14},{8,0},{10,2},{12,4},{14,6},{16,24},{18,... | collective-permute-start | bytes 786440 | tf_op jit(solution)/shard_map/ppermute | solution.py:399
  172.4 12.4 %collective-permute-start.19 = (bf16[64,1024]{1,0:T(8,128)(2,1)S(1)}, bf16[64,1024]{1,0:T(8,128)(2,1)S(1)}, u32[]{:S(2)}, u32[]{:S(2)}) collective-permute-start(bf16[64,1024]{1,0:T(8,128)(2,1)S(1)} %dynamic-slice_bitcast_fusion.4), channel_id=1, source_target_pairs={{0,16},{2,18},{4,20},{6,22},{8,24},{10,26},{12,28},{14,30},{16,0},... | collective-permute-start | bytes 393224 | tf_op jit(solution)/shard_map/ppermute | solution.py:399
  176.6 29.0 %collective-permute-start.12 = (bf16[256,2304]{1,0:T(8,128)(2,1)S(1)}, bf16[256,2304]{1,0:T(8,128)(2,1)S(1)}, u32[]{:S(2)}, u32[]{:S(2)}) collective-permute-start(bf16[256,2304]{1,0:T(8,128)(2,1)S(1)} %bitcast.179), channel_id=1, source_target_pairs={{0,4},{2,6},{4,0},{6,2},{8,12},{10,14},{12,8},{14,10},{16,20},{18,... | collective-permute-start | bytes 3538952 | tf_op jit(solution)/shard_map/ppermute | solution.py:399
  181.7 53.6 %collective-permute-start.21 = (bf16[256,3072]{1,0:T(8,128)(2,1)S(1)}, bf16[256,3072]{1,0:T(8,128)(2,1)S(1)}, u32[]{:S(2)}, u32[]{:S(2)}) collective-permute-start(bf16[256,3072]{1,0:T(8,128)(2,1)S(1)} %bitcast.178), channel_id=1, source_target_pairs={{0,4},{2,6},{4,0},{6,2},{8,12},{10,14},{12,8},{14,10},{16,20},{18,... | collective-permute-start | bytes 4718600 | tf_op jit(solution)/shard_map/ppermute | solution.py:399
  206.0 30.0 %collective-permute-start.13 = (bf16[128,2304]{1,0:T(8,128)(2,1)S(1)}, bf16[128,2304]{1,0:T(8,128)(2,1)S(1)}, u32[]{:S(2)}, u32[]{:S(2)}) collective-permute-start(bf16[128,2304]{1,0:T(8,128)(2,1)S(1)} %bitcast.186), channel_id=1, source_target_pairs={{0,8},{2,10},{4,12},{6,14},{8,0},{10,2},{12,4},{14,6},{16,24},{18,... | collective-permute-start | bytes 1769480 | tf_op jit(solution)/shard_map/ppermute | solution.py:399
  236.2 12.1 %collective-permute-start.14 = (bf16[64,2304]{1,0:T(8,128)(2,1)S(1)}, bf16[64,2304]{1,0:T(8,128)(2,1)S(1)}, u32[]{:S(2)}, u32[]{:S(2)}) collective-permute-start(bf16[64,2304]{1,0:T(8,128)(2,1)S(1)} %dynamic-slice_bitcast_fusion.3), channel_id=1, source_target_pairs={{0,16},{2,18},{4,20},{6,22},{8,24},{10,26},{12,28},{14,30},{16,0},... | collective-permute-start | bytes 884744 | tf_op jit(solution)/shard_map/ppermute | solution.py:399
  238.0 22.0 %collective-permute-start.22 = (bf16[128,3072]{1,0:T(8,128)(2,1)S(1)}, bf16[128,3072]{1,0:T(8,128)(2,1)S(1)}, u32[]{:S(2)}, u32[]{:S(2)}) collective-permute-start(bf16[128,3072]{1,0:T(8,128)(2,1)S(1)} %bitcast.185), channel_id=1, source_target_pairs={{0,8},{2,10},{4,12},{6,14},{8,0},{10,2},{12,4},{14,6},{16,24},{18,... | collective-permute-start | bytes 2359304 | tf_op jit(solution)/shard_map/ppermute | solution.py:399
  249.1 11.3 %collective-permute-start.15 = (bf16[64,384]{1,0:T(8,128)(2,1)S(1)}, bf16[64,384]{1,0:T(8,128)(2,1)S(1)}, u32[]{:S(2)}, u32[]{:S(2)}) collective-permute-start(bf16[64,384]{1,0:T(8,128)(2,1)S(1)} %pad_maximum_fusion.4), channel_id=1, source_target_pairs={{0,1},{1,0},{2,3},{3,2},{4,5},{5,4},{6,7},{7,6},{8,9},{9,8},{10,11... | collective-permute-start | bytes 147464 | tf_op jit(solution)/shard_map/ppermute | solution.py:349
  260.3 16.8 %collective-permute-start.23 = (bf16[64,3072]{1,0:T(8,128)(2,1)S(1)}, bf16[64,3072]{1,0:T(8,128)(2,1)S(1)}, u32[]{:S(2)}, u32[]{:S(2)}) collective-permute-start(bf16[64,3072]{1,0:T(8,128)(2,1)S(1)} %dynamic-slice_bitcast_fusion), channel_id=1, source_target_pairs={{0,16},{2,18},{4,20},{6,22},{8,24},{10,26},{12,28},{14,30},{16,0},... | collective-permute-start | bytes 1179656 | tf_op jit(solution)/shard_map/ppermute | solution.py:399
  (43 other events, 187.4 us)
